TPU v7x, 128 devices: a whole 4x4x4 slice. The times are simulated.
128 devices in a mesh: row: 16 (over z_hi, x, core), col: 8 (over y, z_lo).
Axes of the slice: x: 4, y: 4, z: 4 (z_hi: 2, z_lo: 2; z = z_hi * 2 + z_lo), core: 2. Of those that a mesh axis runs over, the one named last changes fastest.
Arguments:
- tokens: bfloat16 [2, 4096, 2048], P(None, 'row', 'col'), may hold values from -6 to 6
- out_grad: bfloat16 [2, 4096, 2048], P(None, 'row', 'col'), may hold values from -6 to 6
- parents: int32 [2, 13], replicated, may hold values from 0 to 11, as said below
- routes: int32 [2, 4096, 6], P(None, 'row'), may hold values from 0 to 7, all different within a row; in each aligned block of 256 rows (0 to 255, 256 to 511, ..., all dimensions but the last counted through in order) at most 256 rows name the same one
- gates: float32 [2, 4096, 6], P(None, 'row'), may hold values from 0.2 to 1
- norm_in: bfloat16 [2048], replicated, may hold values from 0.5 to 1.5
- w_query: bfloat16 [2048, 3072], P('row', 'col'), may hold values from -0.125 to 0.125
- w_latent: bfloat16 [2048, 576], P('row', 'col'), may hold values from -0.125 to 0.125
- norm_latent: bfloat16 [512], replicated, may hold values from 0.5 to 1.5
- w_expand: bfloat16 [512, 4096], P('row', 'col'), may hold values from -0.25 to 0.25
- w_output: bfloat16 [2048, 2048], P('col', 'row'), may hold values from -4 to 4
- norm_mid: bfloat16 [2048], replicated, may hold values from 0.5 to 1.5
- w_shared_gate: bfloat16 [2048, 2816], P('row', 'col'), may hold values from -0.125 to 0.125
- w_shared_up: bfloat16 [2048, 2816], P('row', 'col'), may hold values from -0.125 to 0.125
- w_shared_down: bfloat16 [2816, 2048], P('col', 'row'), may hold values from -0.109375 to 0.109375
- w_expert_gate: bfloat16 [8, 2048, 1408], P(None, 'row', 'col'), may hold values from -0.125 to 0.125
- w_expert_up: bfloat16 [8, 2048, 1408], P(None, 'row', 'col'), may hold values from -0.125 to 0.125
- w_expert_down: bfloat16 [8, 1408, 2048], P(None, 'col', 'row'), may hold values from -0.15625 to 0.15625
Outputs:
- layer_out: bfloat16 [2, 4096, 2048], P(None, 'row', 'col')
- input_grad: bfloat16 [2, 4096, 2048], P(None, 'row', 'col')
- grad_norm_in: float32 [2048], replicated
- grad_query: float32 [2048, 3072], P('row', 'col')
- grad_latent: float32 [2048, 576], P('row', 'col')
- grad_norm_latent: float32 [512], replicated
- grad_expand: float32 [512, 4096], P('row', 'col')
- grad_output: float32 [2048, 2048], P('col', 'row')
- grad_norm_mid: float32 [2048], replicated
- grad_shared_gate: float32 [2048, 2816], P('row', 'col')
- grad_shared_up: float32 [2048, 2816], P('row', 'col')
- grad_shared_down: float32 [2816, 2048], P('col', 'row')
- grad_expert_gate: float32 [8, 2048, 1408], P(None, 'row', 'col')
- grad_expert_up: float32 [8, 2048, 1408], P(None, 'row', 'col')
- grad_expert_down: float32 [8, 1408, 2048], P(None, 'col', 'row')
Inputs may be any that keep to these rules, and one draw needn't show every extreme that they name: parents[m, 0] is 0 for the trunk, segment 0, which holds tokens 0 to 1023; segment s >= 1 holds the 256 tokens from 1024 + (s - 1) * 256 on, and parents[m, s] is a segment below s; the last segment's parent is segment 13 - 2. `routes`: each row names 6 different experts; of the 256 tokens of a tree held by one index of row (aligned blocks of 256 rows), no expert is named by more than 256.
All inputs are finite; a program needn't handle non-finite values.
Results may differ from a plain program's by a relative error of at most 0.028.
Values may be sent and summed in bfloat16 or wider, within the bound.
No kernel may reach another device: no remote copies, remote signals or barrier semaphores. Data moves between devices by JAX's collectives and lax.ppermute only.
A program may use at most 320 MiB of HBM per device.

v0:
```python
import functools

import jax
import jax.numpy as jnp
from jax import lax
from jax.experimental import pallas as pl
from jax.experimental.pallas import tpu as pltpu
from jax.sharding import PartitionSpec as P

D = 2048
NOPE = 128
ROPE = 64
QK = NOPE + ROPE
VDIM = 128
KVL = 512
TOPK = 6
EXPERTS = 8
MICRO = 2
TRUNK = 1024
BLK = 256
SEGS = 13
ROWS = 16
COLS = 8
TOK = MICRO * BLK
OWN = TOK // COLS
FEAT = D // COLS
QUART = 4
SHARED = 352
ROUTED = 176
HID = 1792
LAT = KVL + ROPE
HALF = BLK // 2
QKP = 256
PACK = VDIM + QKP
WIDE = 3 * HID
LANES = D // ROWS
CUT = LANES // 2
LATC = LAT // COLS
SCALE = QK**-0.5
EPS = 1e-06
THETA = 10000.0
NEG = -1e30
MIB = 1024 * 1024
F32 = jnp.float32
BF16 = jnp.bfloat16
NT = (((1,), (1,)), ((), ()))
TN = (((0,), (0,)), ((), ()))


def inverse_rms(values):
    return lax.rsqrt(jnp.mean(values * values, axis=-1, keepdims=True) + EPS)


def norm_backward(grad_out, values, inv_scale, norm_gain):
    weighted = grad_out * norm_gain
    inner = jnp.mean(weighted * values, axis=-1, keepdims=True)
    return inv_scale * weighted - values * (inv_scale * inv_scale * inv_scale) * inner


def matmul(a, b):
    return jnp.dot(a, b, preferred_element_type=F32)


def matmul_nt(a, b):
    return lax.dot_general(a, b, NT, preferred_element_type=F32)


def matmul_tn(a, b):
    return lax.dot_general(a, b, TN, preferred_element_type=F32)


def swap(values, axis, groups=None):
    return lax.all_to_all(values, axis, 0, 0, tiled=True, axis_index_groups=groups)


def share(values, axis, count):
    return swap(jnp.broadcast_to(values[None], (count,) + values.shape), axis)


def trade(values, axis, mask):
    count = ROWS if axis == "row" else COLS
    return lax.ppermute(values, axis, [(i, i ^ mask) for i in range(count)])


def after(values, *others):
    return lax.optimization_barrier((values,) + others)[0]


def together(*values):
    return lax.optimization_barrier(values)


def smem_values(*values):
    return jnp.stack([jnp.asarray(v, jnp.int32) for v in values])


def pick(values, index, axis=0):
    return lax.dynamic_index_in_dim(values, index, axis, keepdims=False)


def pair_up(shard, axis):
    return jnp.stack([shard, trade(shard, axis, 8 if axis == "row" else 1)])


def ring_up(pair, axis):
    return [pair] + [trade(pair, axis, j << 1) for j in (1, 2, 3)]


def sort_rows_kernel(own_ref, near_ref, far_ref, out_ref):
    for core, ref in ((0, near_ref), (1, far_ref)):
        for x in range(4):
            for z in range(2):
                out_ref[own_ref[0] ^ (8 * z + 2 * x + core)] = ref[x, z]


def finish_rows(ring, row):
    near = jnp.stack(ring)
    far = trade(near, "row", 1)
    vmem = pl.BlockSpec(memory_space=pltpu.VMEM)
    out = pl.pallas_call(
        sort_rows_kernel,
        out_shape=jax.ShapeDtypeStruct((ROWS,) + near.shape[2:], near.dtype),
        in_specs=[pl.BlockSpec(memory_space=pltpu.SMEM), vmem, vmem],
        out_specs=vmem,
        compiler_params=pltpu.CompilerParams(vmem_limit_bytes=16 * MIB),
        cost_estimate=pl.CostEstimate(flops=0, bytes_accessed=near.size, transcendentals=0),
    )(smem_values(row), near, far)
    return out.reshape(D, near.shape[3])


def place_of(apart):
    return ((apart & 1) << 3) | ((apart >> 3) << 2) | ((apart >> 1) & 3)


def lanes(at):
    return pl.ds(pl.multiple_of(at * LANES, LANES), LANES)


def features_kernel(own_ref, blocks_ref, out_ref, out_t_ref):
    for c in range(COLS):
        out_ref[:, c * FEAT : (c + 1) * FEAT] = blocks_ref[c]
    for r in range(ROWS):
        block = blocks_ref[r // 2, :, (r % 2) * LANES : (r % 2 + 1) * LANES]
        out_t_ref[lanes(place_of(own_ref[0] ^ r)), :] = block.T


def features(row, blocks):
    vmem = pl.BlockSpec(memory_space=pltpu.VMEM)
    return pl.pallas_call(
        features_kernel,
        out_shape=(
            jax.ShapeDtypeStruct((TOK, D), BF16),
            jax.ShapeDtypeStruct((D, TOK), BF16),
        ),
        in_specs=[pl.BlockSpec(memory_space=pltpu.SMEM), vmem],
        out_specs=(vmem, vmem),
        compiler_params=pltpu.CompilerParams(vmem_limit_bytes=60 * MIB),
        cost_estimate=pl.CostEstimate(flops=0, bytes_accessed=MIB, transcendentals=0),
    )(smem_values(row), blocks)


def near_shards(shard):
    return trade(shard, "row", 2), trade(shard, "row", 6)


def cut_near(near):
    return near[1][:CUT], near[0][CUT:]


def far_halves(parts):
    return trade(parts[0], "row", 2), trade(parts[1], "row", 6)


def put_kernel(places, own_ref, *refs):
    out_ref, sems = refs[-2:]
    copies = []
    for i, (apart, first) in enumerate(places):
        at = (own_ref[0] ^ apart) * LANES + first
        rows = pl.ds(pl.multiple_of(at, CUT), refs[i].shape[0])
        copy = pltpu.make_async_copy(refs[i], out_ref.at[rows], sems.at[i])
        copy.start()
        copies.append(copy)
    for copy in copies:
        copy.wait()


def put_shards(row, whole, pieces):
    values = [piece for piece, _, _ in pieces]
    places = [(apart, first) for _, apart, first in pieces]
    fresh = whole is None
    return pl.pallas_call(
        functools.partial(put_kernel, places),
        out_shape=jax.ShapeDtypeStruct((D, WIDE), BF16),
        in_specs=[pl.BlockSpec(memory_space=pltpu.SMEM)]
        + [pl.BlockSpec(memory_space=pltpu.VMEM)] * len(values)
        + ([] if fresh else [pl.BlockSpec(memory_space=pl.ANY)]),
        out_specs=pl.BlockSpec(memory_space=pl.ANY),
        scratch_shapes=[pltpu.SemaphoreType.DMA((len(values),))],
        input_output_aliases={} if fresh else {1 + len(values): 0},
        compiler_params=pltpu.CompilerParams(vmem_limit_bytes=60 * MIB),
        cost_estimate=pl.CostEstimate(flops=0, bytes_accessed=MIB, transcendentals=0),
    )(smem_values(row), *values, *([] if fresh else [whole]))


def sum_opposite(blocks):
    return trade(blocks[2], "row", 2), trade(blocks[3], "row", 6)


def add_low(a, b):
    return (a.astype(F32) + b.astype(F32)).astype(BF16)


def sides_kernel(b1_ref, b3_ref, h1_ref, h3_ref, left_ref, right_ref):
    left_ref[:CUT] = b1_ref[:CUT]
    left_ref[CUT:] = (b1_ref[CUT:].astype(F32) + h3_ref[...].astype(F32)).astype(BF16)
    right_ref[:CUT] = (b3_ref[:CUT].astype(F32) + h1_ref[...].astype(F32)).astype(BF16)
    right_ref[CUT:] = b3_ref[CUT:]


def with_opposite(blocks, halves):
    return pl.pallas_call(
        sides_kernel,
        out_shape=[jax.ShapeDtypeStruct((LANES, WIDE), BF16)] * 2,
        compiler_params=pltpu.CompilerParams(vmem_limit_bytes=60 * MIB),
        cost_estimate=pl.CostEstimate(flops=0, bytes_accessed=MIB, transcendentals=0),
    )(blocks[1], blocks[4], *halves)


def sum_neighbours(sides):
    return trade(sides[0], "row", 2), trade(sides[1], "row", 6)


def reduce_x(blocks, j):
    blocks = blocks.reshape((4, 2) + blocks.shape[1:])
    return trade(blocks[j], "row", j << 1) if j else blocks[0]


def reduce_z(*packs):
    sums = []
    for parts in packs:
        parts = [part.astype(F32) for part in parts]
        sums.append(parts[0] + parts[1] + (parts[2] + parts[3]))
    blocks = jnp.concatenate(sums, axis=-1).astype(BF16)
    return blocks[0].astype(F32) + trade(blocks[1], "row", 8).astype(F32)


def attn_grads_kernel(own_ref, x_ref, dq_ref, low_ref, att_ref, keep_ref, send_ref, out):
    out[:, :384] = matmul_tn(x_ref[...], dq_ref[...])
    out[:, 384:] = matmul_tn(low_ref[...], att_ref[...])
    core = own_ref[0] & 1
    keep_ref[0] = out[lanes(core), :].astype(BF16)
    send_ref[0] = out[lanes(1 - core), :].astype(BF16)


def latent_grads_kernel(own_ref, x_ref, dl_ref, lat_ref, de_ref, keep_ref, send_ref, out):
    out[:, 128:] = matmul_tn(x_ref[...], dl_ref[...])
    expand_grad = matmul(lat_ref[...], de_ref[...])
    for half in range(2):
        for i in range(4):
            rows = slice(half * LANES + 32 * i, half * LANES + 32 * (i + 1))
            part = expand_grad[32 * half : 32 * (half + 1), 128 * i : 128 * (i + 1)]
            out[rows, :128] = part
    core = own_ref[0] & 1
    keep_ref[0] = out[lanes(core), :].astype(BF16)
    send_ref[0] = out[lanes(1 - core), :].astype(BF16)


def place_pair(i, own):
    apart = i ^ (own[0] >> 1)
    return (apart & 3) * 2 + (apart >> 2), 0, 0


def weight_grad_pairs(kernel, width, row, ins, specs):
    block = pl.BlockSpec((1, LANES, width), place_pair)
    return pl.pallas_call(
        kernel,
        out_shape=[jax.ShapeDtypeStruct((ROWS // 2, LANES, width), BF16)] * 2,
        grid_spec=pltpu.PrefetchScalarGridSpec(
            num_scalar_prefetch=1,
            grid=(ROWS // 2,),
            in_specs=specs,
            out_specs=[block, block],
            scratch_shapes=[pltpu.VMEM((2 * LANES, width), F32)],
        ),
        compiler_params=pltpu.CompilerParams(vmem_limit_bytes=60 * MIB),
        cost_estimate=pl.CostEstimate(flops=TOK * D * 16, bytes_accessed=MIB, transcendentals=0),
    )(smem_values(row), *ins)


def whole_block(values):
    return pl.BlockSpec(values.shape, lambda i, own: (0, 0))


def attn_weight_grads(row, normed, d_query, d_low, attended):
    columns = pl.BlockSpec((TOK, 2 * LANES), lambda i, own: (0, i))
    specs = [columns, whole_block(d_query), columns, whole_block(attended)]
    ins = (normed, d_query, d_low, attended)
    return weight_grad_pairs(attn_grads_kernel, 640, row, ins, specs)


def latent_weight_grads(row, normed, d_latent, latent_t, d_expanded):
    columns = pl.BlockSpec((TOK, 2 * LANES), lambda i, own: (0, i))
    lines = pl.BlockSpec((2 * KVL // ROWS, TOK), lambda i, own: (i, 0))
    specs = [columns, whole_block(d_latent), lines, whole_block(d_expanded)]
    ins = (normed, d_latent, latent_t, d_expanded)
    return weight_grad_pairs(latent_grads_kernel, 256, row, ins, specs)


def collect_y(blocks, y, j):
    blocks = blocks.reshape((4, 2) + blocks.shape[1:])
    return trade(pick(blocks, y ^ j), "col", j << 1) if j else pick(blocks, y)


def collect_z(blocks, z):
    blocks = [block.astype(F32) for block in blocks]
    blocks = (blocks[0] + blocks[1] + (blocks[2] + blocks[3])).astype(BF16)
    got = trade(pick(blocks, 1 - z), "col", 1)
    return pick(blocks, z).astype(F32) + got.astype(F32)


def trade_quarter(blocks):
    return [blocks[0]] + [trade(blocks[j], "row", j << 2) for j in (1, 2, 3)]


def depth_kernel(parents_ref, seg_ref, out_ref):
    seg = seg_ref[0]
    for m in range(MICRO):

        def climb(step, state):
            at, count = state
            return parents_ref[m, at], count + (at > 0).astype(jnp.int32)

        _, count = lax.fori_loop(0, SEGS, climb, (parents_ref[m, seg], jnp.int32(0)))
        out_ref[m] = count


def ancestor_depths(parents, seg):
    smem = pl.BlockSpec(memory_space=pltpu.SMEM)
    return pl.pallas_call(
        depth_kernel,
        out_shape=jax.ShapeDtypeStruct((MICRO,), jnp.int32),
        in_specs=[smem, smem],
        out_specs=smem,
    )(parents, seg)


def list_ancestors(meta, qb, listed):
    def climb(step, state):
        at, count = state
        listed[count] = at + 3
        return meta[at], count + (at > 0).astype(jnp.int32)

    _, count = lax.fori_loop(0, SEGS, climb, (meta[qb - 3], jnp.int32(0)))
    return count


def causal_mask():
    key = lax.broadcasted_iota(jnp.int32, (BLK, BLK), 0)
    query = lax.broadcasted_iota(jnp.int32, (BLK, BLK), 1)
    return key <= query


def join_halves(meta, near_ref, far_ref, pack):
    core = meta[SEGS] % 2
    pack[:, pl.ds(pl.multiple_of(core * HALF, HALF), HALF), :] = near_ref[...]
    pack[:, pl.ds(pl.multiple_of((1 - core) * HALF, HALF), HALF), :] = far_ref[...]


def attend_kernel(meta, q0, q1, q2, q3, near_ref, far_ref, o0, o1, o2, o3, lse_ref, *scratch):
    q_ref, o_ref, pack, listed = scratch
    quarter, own = meta[SEGS], meta[SEGS + 1]
    join_halves(meta, near_ref, far_ref, pack)
    for j, ref in enumerate((q0, q1, q2, q3)):
        q_ref[own ^ j] = ref[...]
    for i in range(QUART):
        qb = QUART * i + quarter
        q = q_ref[i]
        s = matmul_nt(pack[qb, :, VDIM:], q) * SCALE
        s = jnp.where(causal_mask(), s, NEG)
        top = jnp.max(s, axis=0, keepdims=True)
        p = jnp.exp(s - top)
        total = jnp.sum(p, axis=0, keepdims=True)
        out = matmul_tn(pack[qb, :, :VDIM], p.astype(BF16))

        def visit(block, state):
            top, total, out = state
            s = matmul_nt(block[:, VDIM:], q) * SCALE
            new_top = jnp.maximum(top, jnp.max(s, axis=0, keepdims=True))
            shrink = jnp.exp(top - new_top)
            p = jnp.exp(s - new_top)
            total = total * shrink + jnp.sum(p, axis=0, keepdims=True)
            out = out * shrink + matmul_tn(block[:, :VDIM], p.astype(BF16))
            return new_top, total, out

        def step(kb, state):
            return visit(pack[kb], state)

        state = (top, total, out)
        if i == 0:
            state = lax.fori_loop(0, quarter, step, state)
        else:
            state = visit(pack[: TRUNK // BLK].reshape(TRUNK, PACK), state)
            count = list_ancestors(meta, qb, listed)
            state = lax.fori_loop(0, count, lambda t, c: step(listed[t], c), state)
        top, total, out = state
        o_ref[i] = (out * (1.0 / total)).T.astype(BF16)
        lse_ref[i] = top + jnp.log(total)
    for j, ref in enumerate((o0, o1, o2, o3)):
        ref[...] = o_ref[own ^ j]


def attend(meta, q, near, far):
    smem = pl.BlockSpec(memory_space=pltpu.SMEM)
    vmem = pl.BlockSpec(memory_space=pltpu.VMEM)
    pairs = 32 * BLK * BLK
    return pl.pallas_call(
        attend_kernel,
        out_shape=[jax.ShapeDtypeStruct((BLK, VDIM), BF16)] * QUART
        + [jax.ShapeDtypeStruct((QUART, 1, BLK), F32)],
        in_specs=[smem] + [vmem] * 6,
        out_specs=[vmem] * 5,
        scratch_shapes=[
            pltpu.VMEM((QUART, BLK, QKP), BF16),
            pltpu.VMEM((QUART, BLK, VDIM), BF16),
            pltpu.VMEM((ROWS, BLK, PACK), BF16),
            pltpu.SMEM((16,), jnp.int32),
        ],
        compiler_params=pltpu.CompilerParams(vmem_limit_bytes=60 * MIB),
        cost_estimate=pl.CostEstimate(
            flops=pairs * 2 * (QK + VDIM), bytes_accessed=4 * MIB, transcendentals=pairs
        ),
    )(meta, *q, near, far)


def attend_back_kernel(meta, *refs):
    ins, outs, scratch = refs[:15], refs[15:21], refs[21:]
    near_ref, far_ref, lse_ref = ins[12:]
    keep_ref, send_ref = outs[4:]
    q_ref, o_ref, do_ref, dq_ref, pack, dk, dv, listed = scratch
    quarter, own = meta[SEGS], meta[SEGS + 1]
    core = quarter % 2
    join_halves(meta, near_ref, far_ref, pack)
    for j in range(QUART):
        q_ref[own ^ j] = ins[j][...]
        o_ref[own ^ j] = ins[QUART + j][...]
        do_ref[own ^ j] = ins[2 * QUART + j][...]
    dk[...] = jnp.zeros_like(dk)
    dv[...] = jnp.zeros_like(dv)
    for i in range(QUART):
        qb = QUART * i + quarter
        q = q_ref[i]
        do = do_ref[i]
        lse = lse_ref[i]
        pairs = do.astype(F32) * o_ref[i].astype(F32)
        delta = jnp.sum(pairs.T, axis=0, keepdims=True)

        def trunk(dqt):
            block = pack[: TRUNK // BLK].reshape(TRUNK, PACK)
            key = block[:, VDIM:]
            p = jnp.exp(matmul_nt(key, q) * SCALE - lse)
            dp = matmul_nt(block[:, :VDIM], do)
            ds = (p * (dp - delta) * SCALE).astype(BF16)
            shape = (TRUNK // BLK, BLK, -1)
            dv[: TRUNK // BLK] += matmul(p.astype(BF16), do).reshape(shape)
            dk[: TRUNK // BLK] += matmul(ds, q).reshape(shape)
            return dqt + matmul_tn(key, ds)

        def step(kb, dqt, masked=False):
            key = pack[kb, :, VDIM:]
            s = matmul_nt(key, q) * SCALE
            p = jnp.exp(s - lse)
            if masked:
                p = jnp.where(causal_mask(), p, 0.0)
            dp = matmul_nt(pack[kb, :, :VDIM], do)
            ds = (p * (dp - delta) * SCALE).astype(BF16)
            dv[kb] += matmul(p.astype(BF16), do)
            dk[kb] += matmul(ds, q)
            return dqt + matmul_tn(key, ds)

        dqt = step(qb, jnp.zeros((QKP, BLK), F32), True)
        if i == 0:
            dqt = lax.fori_loop(0, quarter, step, dqt)
        else:
            dqt = trunk(dqt)
            count = list_ancestors(meta, qb, listed)
            dqt = lax.fori_loop(0, count, lambda t, c: step(listed[t], c), dqt)
        dq_ref[i] = dqt.T.astype(BF16)
    for j in range(QUART):
        outs[j][...] = dq_ref[own ^ j]
    for half, ref in ((core, keep_ref), (1 - core, send_ref)):
        part = pl.ds(pl.multiple_of(half * HALF, HALF), HALF)
        ref[:, :, :VDIM] = dv[:, part, :].astype(BF16)
        ref[:, :, VDIM:] = dk[:, part, :].astype(BF16)


def attend_back(meta, q, o, d_o, near, far, lse):
    smem = pl.BlockSpec(memory_space=pltpu.SMEM)
    vmem = pl.BlockSpec(memory_space=pltpu.VMEM)
    pairs = 32 * BLK * BLK
    return pl.pallas_call(
        attend_back_kernel,
        out_shape=[jax.ShapeDtypeStruct((BLK, QKP), BF16)] * QUART
        + [jax.ShapeDtypeStruct((ROWS, HALF, PACK), BF16)] * 2,
        in_specs=[smem] + [vmem] * 15,
        out_specs=[vmem] * 6,
        scratch_shapes=[
            pltpu.VMEM((QUART, BLK, QKP), BF16),
            pltpu.VMEM((QUART, BLK, VDIM), BF16),
            pltpu.VMEM((QUART, BLK, VDIM), BF16),
            pltpu.VMEM((QUART, BLK, QKP), BF16),
            pltpu.VMEM((ROWS, BLK, PACK), BF16),
            pltpu.VMEM((ROWS, BLK, QKP), F32),
            pltpu.VMEM((ROWS, BLK, VDIM), F32),
            pltpu.SMEM((16,), jnp.int32),
        ],
        compiler_params=pltpu.CompilerParams(vmem_limit_bytes=60 * MIB),
        cost_estimate=pl.CostEstimate(
            flops=pairs * 2 * (3 * QK + 2 * VDIM), bytes_accessed=10 * MIB, transcendentals=pairs
        ),
    )(meta, *q, *o, *d_o, near, far, lse)


def project_kernel(own_ref, b0, b1, b2, b3, w_ref, attended_ref, out_ref, blocks):
    for j, ref in enumerate((b0, b1, b2, b3)):
        blocks[own_ref[0] ^ j] = ref[...]
    for h in range(2):
        for m in range(MICRO):
            attended_ref[m * BLK : (m + 1) * BLK, h * VDIM : (h + 1) * VDIM] = blocks[2 * h + m]
    out = matmul_nt(attended_ref[...], w_ref[...]).astype(BF16)
    for c in range(COLS):
        out_ref[c] = out[c * OWN : (c + 1) * OWN]


def project(own, blocks, w_packed):
    def whole(*shape):
        return pl.BlockSpec(shape, lambda i: (0,) * len(shape))

    return pl.pallas_call(
        project_kernel,
        grid=(1,),
        out_shape=(
            jax.ShapeDtypeStruct((TOK, 2 * VDIM), BF16),
            jax.ShapeDtypeStruct((COLS, OWN, D), BF16),
        ),
        in_specs=[pl.BlockSpec(memory_space=pltpu.SMEM)]
        + [whole(BLK, VDIM)] * QUART
        + [pl.BlockSpec((D, 2 * VDIM), lambda i: (0, 2))],
        out_specs=(whole(TOK, 2 * VDIM), whole(COLS, OWN, D)),
        scratch_shapes=[pltpu.VMEM((QUART, BLK, VDIM), BF16)],
        compiler_params=pltpu.CompilerParams(vmem_limit_bytes=60 * MIB),
        cost_estimate=pl.CostEstimate(flops=TOK * D * 512, bytes_accessed=MIB, transcendentals=0),
    )(smem_values(own), *blocks, w_packed)


def project_back_kernel(own_ref, d_ref, w_ref, o0, o1, o2, o3, blocks):
    for c in range(COLS):
        rows = slice((c % QUART) * OWN, (c % QUART + 1) * OWN)
        part = matmul(d_ref[c], w_ref[...]).astype(BF16)
        for h in range(2):
            blocks[2 * h + c // QUART, rows, :] = part[:, h * VDIM : (h + 1) * VDIM]
    for j, ref in enumerate((o0, o1, o2, o3)):
        ref[...] = blocks[own_ref[0] ^ j]


def project_back(own, d_low, w_packed):
    def whole(*shape):
        return pl.BlockSpec(shape, lambda i: (0,) * len(shape))

    return pl.pallas_call(
        project_back_kernel,
        grid=(1,),
        out_shape=[jax.ShapeDtypeStruct((BLK, VDIM), BF16)] * QUART,
        in_specs=[
            pl.BlockSpec(memory_space=pltpu.SMEM),
            whole(COLS, OWN, D),
            pl.BlockSpec((D, 2 * VDIM), lambda i: (0, 2)),
        ],
        out_specs=[whole(BLK, VDIM)] * QUART,
        scratch_shapes=[pltpu.VMEM((QUART, BLK, VDIM), BF16)],
        compiler_params=pltpu.CompilerParams(vmem_limit_bytes=60 * MIB),
        cost_estimate=pl.CostEstimate(flops=TOK * D * 512, bytes_accessed=MIB, transcendentals=0),
    )(smem_values(own), d_low, w_packed)


def front_kernel(col_ref, pieces_ref, gain_ref, wl_ref, x_ref, normed_ref, scale_ref, lat_ref):
    for y in range(4):
        for z in range(2):
            at = (2 * y + (z ^ (col_ref[0] & 1))) * FEAT
            x_ref[:, pl.ds(pl.multiple_of(at, FEAT), FEAT)] = pieces_ref[y, z]
    x = x_ref[...].astype(F32)
    scale = inverse_rms(x)
    scale_ref[...] = scale
    normed = (x * scale * gain_ref[...]).astype(BF16)
    normed_ref[...] = normed
    latent = matmul(normed, wl_ref[...]).T[:LATC].astype(BF16)
    for c in range(COLS):
        lat_ref[c] = latent


def front(col, pieces, gain, w_packed):
    rows = 128
    return pl.pallas_call(
        front_kernel,
        grid=(TOK // rows,),
        out_shape=(
            jax.ShapeDtypeStruct((TOK, D), BF16),
            jax.ShapeDtypeStruct((TOK, D), BF16),
            jax.ShapeDtypeStruct((TOK, 1), F32),
            jax.ShapeDtypeStruct((COLS, LATC, TOK), BF16),
        ),
        in_specs=[
            pl.BlockSpec(memory_space=pltpu.SMEM),
            pl.BlockSpec((4, 2, rows, FEAT), lambda j: (0, 0, j, 0)),
            pl.BlockSpec((1, D), lambda j: (0, 0)),
            pl.BlockSpec((D, 128), lambda j: (0, 6)),
        ],
        out_specs=(
            pl.BlockSpec((rows, D), lambda j: (j, 0)),
            pl.BlockSpec((rows, D), lambda j: (j, 0)),
            pl.BlockSpec((rows, 1), lambda j: (j, 0)),
            pl.BlockSpec((COLS, LATC, rows), lambda j: (0, 0, j)),
        ),
        compiler_params=pltpu.CompilerParams(vmem_limit_bytes=60 * MIB),
        cost_estimate=pl.CostEstimate(flops=TOK * D * 256, bytes_accessed=MIB, transcendentals=0),
    )(smem_values(col), pieces, gain.reshape(1, D), w_packed)


def half_turn():
    source = lax.broadcasted_iota(jnp.int32, (2 * ROPE, 2 * ROPE), 0)
    target = lax.broadcasted_iota(jnp.int32, (2 * ROPE, 2 * ROPE), 1)
    half = ROPE // 2
    first = target % ROPE < half
    value = jnp.where(
        first & (source == target + half),
        -1.0,
        jnp.where((target % ROPE >= half) & (source == target - half), 1.0, 0.0),
    )
    return value.astype(BF16)


def query_kernel(own_ref, normed_ref, w_ref, cos_ref, sin_ref, o0, o1, o2, o3, blocks):
    normed = normed_ref[...]
    w_rope = w_ref[:, 2 * NOPE :]
    turned = matmul(w_rope, half_turn()).astype(BF16)
    rope = matmul(normed, w_rope) * cos_ref[...] + matmul(normed, turned) * sin_ref[...]
    rope = rope.astype(BF16)
    nope = matmul(normed, w_ref[:, : 2 * NOPE]).astype(BF16)
    blank = jnp.zeros((BLK, QKP - QK), BF16)
    for h in range(2):
        for m in range(MICRO):
            rows = slice(m * BLK, (m + 1) * BLK)
            blocks[2 * h + m, :, :NOPE] = nope[rows, h * NOPE : (h + 1) * NOPE]
            blocks[2 * h + m, :, NOPE:QK] = rope[rows, h * ROPE : (h + 1) * ROPE]
            blocks[2 * h + m, :, QK:] = blank
    for j, ref in enumerate((o0, o1, o2, o3)):
        ref[...] = blocks[own_ref[0] ^ j]


def project_query(own, normed, w_packed, cos_wide, sin_wide):
    def whole(shape):
        return pl.BlockSpec(shape, lambda i: (0, 0))

    return pl.pallas_call(
        query_kernel,
        grid=(1,),
        out_shape=[jax.ShapeDtypeStruct((BLK, QKP), BF16)] * QUART,
        in_specs=[
            pl.BlockSpec(memory_space=pltpu.SMEM),
            whole((TOK, D)),
            whole((D, 2 * QK)),
            whole((TOK, 2 * ROPE)),
            whole((TOK, 2 * ROPE)),
        ],
        out_specs=[whole((BLK, QKP))] * QUART,
        scratch_shapes=[pltpu.VMEM((QUART, BLK, QKP), BF16)],
        compiler_params=pltpu.CompilerParams(vmem_limit_bytes=60 * MIB),
        cost_estimate=pl.CostEstimate(flops=TOK * D * 256, bytes_accessed=MIB, transcendentals=0),
    )(smem_values(own), normed, w_packed, cos_wide, sin_wide)


def query_back_kernel(own_ref, b0, b1, b2, b3, cos_ref, sin_ref, out_ref, blocks):
    turn = half_turn()
    for j, ref in enumerate((b0, b1, b2, b3)):
        blocks[own_ref[0] ^ j] = ref[...]
    for m in range(MICRO):
        rows = slice(m * BLK, (m + 1) * BLK)
        for h in range(2):
            out_ref[rows, h * NOPE : (h + 1) * NOPE] = blocks[2 * h + m, :, :NOPE]
        rope = jnp.concatenate([blocks[m, :, NOPE:QK], blocks[2 + m, :, NOPE:QK]], axis=1)
        rope = rope.astype(F32) * cos_ref[rows, :] + matmul_nt(rope, turn) * sin_ref[rows, :]
        out_ref[rows, 2 * NOPE :] = rope.astype(BF16)


def query_back(own, blocks, cos_wide, sin_wide):
    vmem = pl.BlockSpec(memory_space=pltpu.VMEM)
    return pl.pallas_call(
        query_back_kernel,
        out_shape=jax.ShapeDtypeStruct((TOK, 2 * QK), BF16),
        in_specs=[pl.BlockSpec(memory_space=pltpu.SMEM)] + [vmem] * 6,
        out_specs=vmem,
        scratch_shapes=[pltpu.VMEM((QUART, BLK, QKP), BF16)],
        compiler_params=pltpu.CompilerParams(vmem_limit_bytes=60 * MIB),
        cost_estimate=pl.CostEstimate(flops=TOK * D * 16, bytes_accessed=MIB, transcendentals=0),
    )(smem_values(own), *blocks, cos_wide, sin_wide)


def expand_kernel(latent_ref, cos_ref, sin_ref, gain_ref, w_ref, normed_ref, out_ref):
    c = latent_ref[:KVL, :].astype(F32)
    scale = lax.rsqrt(jnp.mean(c * c, axis=0, keepdims=True) + EPS)
    normed = (c * scale * gain_ref[...]).astype(BF16)
    normed_ref[...] = normed
    expanded = matmul_tn(normed, w_ref[...]).astype(BF16)
    half = ROPE // 2
    a = latent_ref[KVL : KVL + half, :].astype(F32)
    b = latent_ref[KVL + half :, :].astype(F32)
    cos, sin = cos_ref[...], sin_ref[...]
    rope = jnp.concatenate(
        [a * cos - b * sin, a * sin + b * cos, jnp.zeros((QKP - QK, TOK), F32)], axis=0
    )
    rope = rope.T.astype(BF16)
    for h in range(2):
        key = h * (NOPE + VDIM)
        value = key + NOPE
        for m in range(MICRO):
            for core in range(2):
                rows = slice(m * BLK + core * HALF, m * BLK + (core + 1) * HALF)
                for chip in range(2):
                    at = 8 * h + 4 * m + 2 * chip + core
                    out_ref[at, :, :VDIM] = expanded[rows, value : value + VDIM]
                    out_ref[at, :, VDIM : VDIM + NOPE] = expanded[rows, key : key + NOPE]
                    out_ref[at, :, VDIM + NOPE :] = rope[rows, :]


def expand(latent_t, cos_t, sin_t, gain, w_expand):
    return pl.pallas_call(
        expand_kernel,
        out_shape=(
            jax.ShapeDtypeStruct((KVL, TOK), BF16),
            jax.ShapeDtypeStruct((ROWS, HALF, PACK), BF16),
        ),
        compiler_params=pltpu.CompilerParams(vmem_limit_bytes=24 * MIB),
        cost_estimate=pl.CostEstimate(flops=TOK * D * 256, bytes_accessed=MIB, transcendentals=0),
    )(latent_t, cos_t, sin_t, gain.reshape(KVL, 1), w_expand)


def latent_back_kernel(
    pack_ref, latent_ref, cos_ref, sin_ref, gain_ref, w_ref, d_exp_ref, d_latent_ref, gg_ref
):
    rope = [None] * (2 * MICRO)
    for h in range(2):
        for m in range(MICRO):
            for core in range(2):
                at = 8 * h + 4 * m + core
                part = pack_ref[at].astype(F32) + pack_ref[at + 2].astype(F32)
                rows = slice(m * BLK + core * HALF, m * BLK + (core + 1) * HALF)
                key = h * (NOPE + VDIM)
                d_exp_ref[rows, key : key + NOPE] = part[:, VDIM : VDIM + NOPE].astype(BF16)
                d_exp_ref[rows, key + NOPE : key + NOPE + VDIM] = part[:, :VDIM].astype(BF16)
                piece = part[:, VDIM + NOPE :]
                at = 2 * m + core
                rope[at] = piece if h == 0 else rope[at] + piece
    rope = jnp.concatenate(rope, axis=0).T
    half = ROPE // 2
    a, b = rope[:half], rope[half:ROPE]
    cos, sin = cos_ref[...], sin_ref[...]
    d_latent_ref[KVL : KVL + half, :] = (a * cos + b * sin).astype(BF16)
    d_latent_ref[KVL + half :, :] = (b * cos - a * sin).astype(BF16)
    d_normed = matmul_nt(w_ref[...], d_exp_ref[...])
    c = latent_ref[:KVL, :].astype(F32)
    scale = lax.rsqrt(jnp.mean(c * c, axis=0, keepdims=True) + EPS)
    gg_ref[...] = jnp.sum(d_normed * c * scale, axis=1, keepdims=True)
    weighted = d_normed * gain_ref[...]
    inner = jnp.mean(weighted * c, axis=0, keepdims=True)
    d_latent_ref[:KVL, :] = (scale * weighted - c * (scale * scale * scale) * inner).astype(BF16)


def latent_back(pack, latent_t, cos_t, sin_t, gain, w_expand):
    return pl.pallas_call(
        latent_back_kernel,
        out_shape=(
            jax.ShapeDtypeStruct((TOK, 2 * (NOPE + VDIM)), BF16),
            jax.ShapeDtypeStruct((LAT, TOK), BF16),
            jax.ShapeDtypeStruct((KVL, 1), F32),
        ),
        compiler_params=pltpu.CompilerParams(vmem_limit_bytes=60 * MIB),
        cost_estimate=pl.CostEstimate(flops=TOK * D * 256, bytes_accessed=MIB, transcendentals=0),
    )(pack, latent_t, cos_t, sin_t, gain.reshape(KVL, 1), w_expand)


def hidden_kernel(
    own_ref, mid_ref, grad_ref, gate_ref, spread_ref, wg_ref, wu_ref, wd_ref, out_ref, turned_ref
):
    mid = mid_ref[...]
    pre = matmul(mid, wg_ref[...])
    up = matmul(mid, wu_ref[...])
    back = matmul(grad_ref[...], wd_ref[...])
    gate = matmul(gate_ref[...], spread_ref[...])
    sig = 0.5 + 0.5 * jnp.tanh(0.5 * pre)
    act = pre * sig
    back = back * gate
    out_ref[0] = (back * up * (sig * (1.0 + pre * (1.0 - sig)))).astype(BF16)
    out_ref[1] = (back * act).astype(BF16)
    out_ref[2] = (act * up * gate).astype(BF16)
    for i in range(3):
        r = jnp.minimum(3 * pl.program_id(0) + i, ROWS - 1)
        turned_ref[lanes(place_of(own_ref[0] ^ r)), :] = mid_ref[:, lanes(r)].T


def hidden(row, mid, grad, gates, spread, weights):
    whole = pl.BlockSpec((TOK, D), lambda j: (0, 0))
    parts = HID // BLK

    def weight(at):
        return pl.BlockSpec((D, BLK), lambda j: (0, at * parts + j))

    return pl.pallas_call(
        hidden_kernel,
        grid=(parts,),
        out_shape=(
            jax.ShapeDtypeStruct((3, TOK, HID), BF16),
            jax.ShapeDtypeStruct((D, TOK), BF16),
        ),
        in_specs=[
            pl.BlockSpec(memory_space=pltpu.SMEM),
            whole,
            whole,
            pl.BlockSpec(gates.shape, lambda j: (0, 0)),
            pl.BlockSpec((spread.shape[0], BLK), lambda j: (0, j)),
            weight(0),
            weight(1),
            weight(2),
        ],
        out_specs=(
            pl.BlockSpec((3, TOK, BLK), lambda j: (0, 0, j)),
            pl.BlockSpec((D, TOK), lambda j: (0, 0)),
        ),
        compiler_params=pltpu.CompilerParams(vmem_limit_bytes=60 * MIB),
        cost_estimate=pl.CostEstimate(
            flops=2 * TOK * D * HID * 3, bytes_accessed=32 * MIB, transcendentals=TOK * HID
        ),
    )(smem_values(row), mid, grad, gates, spread, weights, weights, weights)


def mid_grad_kernel(hid_ref, w_ref, out_ref):
    out = matmul_nt(hid_ref[0], w_ref[:, :HID]) + matmul_nt(hid_ref[1], w_ref[:, HID:])
    out_ref[...] = out.astype(BF16)


def mid_grad(hid, weights):
    return pl.pallas_call(
        mid_grad_kernel,
        grid=(4,),
        out_shape=jax.ShapeDtypeStruct((TOK, D), BF16),
        in_specs=[
            pl.BlockSpec((2, TOK, HID), lambda j: (0, 0, 0)),
            pl.BlockSpec((D // 4, 2 * HID), lambda j: (j, 0)),
        ],
        out_specs=pl.BlockSpec((TOK, D // 4), lambda j: (0, j)),
        compiler_params=pltpu.CompilerParams(vmem_limit_bytes=60 * MIB),
        cost_estimate=pl.CostEstimate(
            flops=2 * TOK * D * HID * 2, bytes_accessed=20 * MIB, transcendentals=0
        ),
    )(hid, weights)


def output_kernel(col_ref, hid_ref, w_ref, residual_ref, out_ref):
    out_ref[0] = matmul_nt(hid_ref[0], w_ref[...]).astype(BF16)
    own = pl.ds(pl.multiple_of(col_ref[0] * OWN, OWN), OWN)
    out_ref[0, own, :] = (
        matmul_nt(hid_ref[0, own, :], w_ref[...]) + residual_ref[...]
    ).astype(BF16)


def output(col, hid, weights, residual):
    return pl.pallas_call(
        output_kernel,
        grid=(COLS,),
        out_shape=jax.ShapeDtypeStruct((COLS, TOK, FEAT), BF16),
        in_specs=[
            pl.BlockSpec(memory_space=pltpu.SMEM),
            pl.BlockSpec((1, TOK, HID), lambda j: (2, 0, 0)),
            pl.BlockSpec((FEAT, HID), lambda j: (j, 2)),
            pl.BlockSpec((OWN, FEAT), lambda j: (0, j)),
        ],
        out_specs=pl.BlockSpec((1, TOK, FEAT), lambda j: (j, 0, 0)),
        compiler_params=pltpu.CompilerParams(vmem_limit_bytes=60 * MIB),
        cost_estimate=pl.CostEstimate(
            flops=TOK * D * HID // 8, bytes_accessed=MIB, transcendentals=0
        ),
    )(col.astype(jnp.int32).reshape(1), hid, weights, residual)


def mid_kernel(parts_ref, inputs_ref, gain_ref, residual_ref, scale_ref, normed_ref):
    total = inputs_ref[...].astype(F32)
    for c in range(COLS):
        total = total + parts_ref[c].astype(F32)
    scale = inverse_rms(total)
    residual_ref[...] = total
    scale_ref[...] = scale
    normed = (total * scale * gain_ref[...]).astype(BF16)
    for c in range(COLS):
        normed_ref[c] = normed


def mid(parts, inputs, gain):
    return pl.pallas_call(
        mid_kernel,
        out_shape=(
            jax.ShapeDtypeStruct((OWN, D), F32),
            jax.ShapeDtypeStruct((OWN, 1), F32),
            jax.ShapeDtypeStruct((COLS, OWN, D), BF16),
        ),
        compiler_params=pltpu.CompilerParams(vmem_limit_bytes=20 * MIB),
        cost_estimate=pl.CostEstimate(
            flops=OWN * D * 16, bytes_accessed=5 * MIB, transcendentals=0
        ),
    )(parts, inputs, gain.reshape(1, D))


def mid_back_kernel(
    parts_ref, residual_ref, scale_ref, grad_ref, gain_ref, out_ref, low_ref, gain_grad_ref
):
    d_mid = parts_ref[0].astype(F32)
    for c in range(1, COLS):
        d_mid = d_mid + parts_ref[c].astype(F32)
    residual, scale = residual_ref[...], scale_ref[...]
    gain_grad_ref[...] = jnp.sum(d_mid * residual * scale, axis=0, keepdims=True)
    out = grad_ref[...].astype(F32) + norm_backward(d_mid, residual, scale, gain_ref[...])
    out_ref[...] = out
    low = out.astype(BF16)
    for c in range(COLS):
        low_ref[c] = low


def mid_back(parts, residual, scale, grad, gain):
    return pl.pallas_call(
        mid_back_kernel,
        out_shape=(
            jax.ShapeDtypeStruct((OWN, D), F32),
            jax.ShapeDtypeStruct((COLS, OWN, D), BF16),
            jax.ShapeDtypeStruct((1, D), F32),
        ),
        compiler_params=pltpu.CompilerParams(vmem_limit_bytes=20 * MIB),
        cost_estimate=pl.CostEstimate(
            flops=OWN * D * 24, bytes_accessed=5 * MIB, transcendentals=0
        ),
    )(parts, residual, scale, grad, gain.reshape(1, D))


def input_back_kernel(
    col_ref, dq_ref, dl_ref, wq_ref, wl_ref, x_ref, scale_ref, gain_ref, own_ref, out_ref, gg_ref
):
    step = pl.program_id(0)
    d_in = matmul_nt(dq_ref[...], wq_ref[...]) + matmul_nt(dl_ref[...], wl_ref[...])
    x, scale = x_ref[...].astype(F32), scale_ref[...]
    gain_grad = jnp.sum(d_in * x * scale, axis=0, keepdims=True)

    @pl.when(step == 0)
    def _():
        gg_ref[...] = gain_grad

    @pl.when(step > 0)
    def _():
        gg_ref[...] += gain_grad

    out = norm_backward(d_in, x, scale, gain_ref[...])
    for half in range(2):
        mine = (col_ref[0] == 2 * step + half).astype(F32)
        rows = slice(half * OWN, (half + 1) * OWN)
        part = (out[rows] + mine * own_ref[...]).astype(BF16)
        for c in range(COLS):
            out_ref[c, rows, :] = part[:, c * FEAT : (c + 1) * FEAT]


def input_back(col, d_query, d_latent, w_packed, inputs, scale, gain, own):
    rows = 2 * OWN
    widths = (d_query.shape[1], d_latent.shape[1])
    return pl.pallas_call(
        input_back_kernel,
        grid=(TOK // rows,),
        out_shape=(
            jax.ShapeDtypeStruct((COLS, TOK, FEAT), BF16),
            jax.ShapeDtypeStruct((1, D), F32),
        ),
        in_specs=[
            pl.BlockSpec(memory_space=pltpu.SMEM),
            pl.BlockSpec((rows, widths[0]), lambda j: (j, 0)),
            pl.BlockSpec((rows, widths[1]), lambda j: (j, 0)),
            pl.BlockSpec((D, widths[0]), lambda j: (0, 0)),
            pl.BlockSpec((D, widths[1]), lambda j: (0, 6)),
            pl.BlockSpec((rows, D), lambda j: (j, 0)),
            pl.BlockSpec((rows, 1), lambda j: (j, 0)),
            pl.BlockSpec((1, D), lambda j: (0, 0)),
            pl.BlockSpec((OWN, D), lambda j: (0, 0)),
        ],
        out_specs=(
            pl.BlockSpec((COLS, rows, FEAT), lambda j: (0, j, 0)),
            pl.BlockSpec((1, D), lambda j: (0, 0)),
        ),
        compiler_params=pltpu.CompilerParams(vmem_limit_bytes=60 * MIB),
        cost_estimate=pl.CostEstimate(
            flops=2 * TOK * D * 640, bytes_accessed=9 * MIB, transcendentals=0
        ),
    )(
        smem_values(col),
        d_query,
        d_latent,
        w_packed,
        w_packed,
        inputs,
        scale,
        gain.reshape(1, D),
        own,
    )


def send_grad_kernel(mid_ref, grad_ref, hid_ref, out_ref):
    @pl.when(pl.program_id(0) < 2)
    def _():
        out_ref[...] = matmul(mid_ref[...], hid_ref[0]).astype(BF16)

    @pl.when(pl.program_id(0) == 2)
    def _():
        out_ref[...] = matmul(grad_ref[...], hid_ref[0]).astype(BF16)


def keep_grad_kernel(mid_ref, grad_ref, hid_ref, got_ref, *out_refs):
    def store(lhs_ref):
        out = matmul(lhs_ref[...], hid_ref[0]) + got_ref[...].astype(F32)
        first = 0
        for ref in out_refs:
            rows = ref.shape[0]
            ref[...] = out[first : first + rows].astype(BF16)
            first += rows

    @pl.when(pl.program_id(0) < 2)
    def _():
        store(mid_ref)

    @pl.when(pl.program_id(0) == 2)
    def _():
        store(grad_ref)


def send_grads(z, mid_t, grad_t, hid):
    rows = D // 4
    whole = pl.BlockSpec((rows, TOK), lambda s: (2 + z, 0))
    return pl.pallas_call(
        send_grad_kernel,
        grid=(3,),
        out_shape=jax.ShapeDtypeStruct((rows, WIDE), BF16),
        in_specs=[whole, whole, pl.BlockSpec((1, TOK, HID), lambda s: (s, 0, 0))],
        out_specs=pl.BlockSpec((rows, HID), lambda s: (0, s)),
        compiler_params=pltpu.CompilerParams(vmem_limit_bytes=60 * MIB),
        cost_estimate=pl.CostEstimate(
            flops=TOK * D * HID // 32, bytes_accessed=MIB, transcendentals=0
        ),
    )(mid_t, grad_t, hid)


def keep_grads(z, mid_t, grad_t, hid, got):
    rows = D // 4
    whole = pl.BlockSpec((rows, TOK), lambda s: (z, 0))
    heights = (LANES, LANES, CUT, CUT, LANES)
    return pl.pallas_call(
        keep_grad_kernel,
        grid=(3,),
        out_shape=[jax.ShapeDtypeStruct((height, WIDE), BF16) for height in heights],
        in_specs=[
            whole,
            whole,
            pl.BlockSpec((1, TOK, HID), lambda s: (s, 0, 0)),
            pl.BlockSpec((rows, HID), lambda s: (0, s)),
        ],
        out_specs=[pl.BlockSpec((h, HID), lambda s: (0, s)) for h in heights],
        compiler_params=pltpu.CompilerParams(vmem_limit_bytes=60 * MIB),
        cost_estimate=pl.CostEstimate(
            flops=TOK * D * HID // 32, bytes_accessed=MIB, transcendentals=0
        ),
    )(mid_t, grad_t, hid, got)


def rotary_tables(parents, row):
    seg = jnp.maximum(row - (TRUNK // BLK - 1), 0).astype(jnp.int32)
    depths = ancestor_depths(parents, seg.reshape(1))
    starts = jnp.where(seg > 0, TRUNK + BLK * depths, BLK * row)
    positions = (starts[:, None] + jnp.arange(BLK, dtype=jnp.int32)[None, :]).reshape(TOK)
    frequency = THETA ** (-jnp.arange(ROPE // 2, dtype=F32) / (ROPE // 2))
    angles = positions.astype(F32)[:, None] * frequency[None, :]
    cos_table, sin_table = jnp.cos(angles), jnp.sin(angles)
    cos_wide, sin_wide = jnp.tile(cos_table, (1, 4)), jnp.tile(sin_table, (1, 4))
    return cos_table.T, sin_table.T, cos_wide, sin_wide


def pack_hidden(shared, routed):
    rows = shared.shape[0]
    return jnp.concatenate(
        [
            shared,
            jnp.swapaxes(routed, 0, 1).reshape(rows, EXPERTS * ROUTED),
            jnp.zeros((rows, HID - SHARED - EXPERTS * ROUTED), routed.dtype),
        ],
        axis=1,
    )


def local(
    tokens,
    out_grad,
    parents,
    routes,
    gates,
    norm_in,
    w_query,
    w_latent,
    norm_latent,
    w_expand,
    w_output,
    norm_mid,
    w_shared_gate,
    w_shared_up,
    w_shared_down,
    w_expert_gate,
    w_expert_up,
    w_expert_down,
):
    row = lax.axis_index("row")
    col = lax.axis_index("col")
    group = row // QUART
    own_start = col * OWN
    gain_in = norm_in.astype(F32)
    gain_latent = norm_latent.astype(F32)
    gain_mid = norm_mid.astype(F32)
    heads = 2

    query_pack = w_query.reshape(D // ROWS, heads, QK)
    attn_pack = jnp.concatenate(
        [
            query_pack[:, :, :NOPE].reshape(D // ROWS, heads * NOPE),
            query_pack[:, :, NOPE:].reshape(D // ROWS, heads * ROPE),
            w_expand.reshape(KVL // ROWS, 4, 128).transpose(1, 0, 2).reshape(D // ROWS, 128),
            w_output.T,
            w_latent,
            jnp.zeros((D // ROWS, 128 - LATC), BF16),
        ],
        axis=1,
    )
    ffn_pack = jnp.concatenate(
        [
            pack_hidden(w_shared_gate, w_expert_gate),
            pack_hidden(w_shared_up, w_expert_up),
            pack_hidden(w_shared_down.T, jnp.swapaxes(w_expert_down, 1, 2)),
        ],
        axis=1,
    )
    attn_pair, input_pair, ffn_pack = together(
        pair_up(attn_pack, "row"), pair_up(tokens.reshape(TOK, FEAT), "col"), ffn_pack
    )
    line_groups = [[2 * y + z for y in range(4)] for z in range(2)]
    input_copies = jnp.broadcast_to(input_pair[None], (4,) + input_pair.shape)
    attn_ring, input_ring, ffn_pack, ffn_other, tables = together(
        ring_up(attn_pair, "row"),
        swap(input_copies, "col", line_groups),
        ffn_pack,
        trade(ffn_pack, "row", 8),
        rotary_tables(parents, row),
    )
    cos_t, sin_t, cos_wide, sin_wide = tables
    ffn_near = near_shards(ffn_pack)
    attn_full = finish_rows(attn_ring, row)
    expand_full = attn_full[:, 384:512].reshape(ROWS, 4, KVL // ROWS, 128)
    expand_full = expand_full.transpose(0, 2, 1, 3).reshape(KVL, heads * (NOPE + VDIM))

    inputs, normed_in, scale_in, latent_parts = front(col, input_ring, gain_in, attn_full)
    query = project_query(group, normed_in, attn_full, cos_wide, sin_wide)
    latent_t, query, normed_in, ffn_near = together(
        swap(latent_parts, "col"), query, normed_in, ffn_near
    )
    latent_t = latent_t.reshape(LAT, TOK)
    latent_normed_t, pack = expand(latent_t, cos_t, sin_t, gain_latent, expand_full)
    pack, query, ffn_near, out_grad, ffn_other = together(
        pack, query, ffn_near, out_grad, ffn_other
    )
    near, query, ffn_cut, grad_copies = together(
        swap(pack, "row"),
        trade_quarter(query),
        cut_near(ffn_near),
        jnp.broadcast_to(out_grad.reshape(1, TOK, FEAT), (COLS, TOK, FEAT)),
    )
    grad_ring = swap(grad_copies, "col")
    ffn_far = far_halves(ffn_cut)
    far = trade(near, "row", 1)

    meta = jnp.concatenate([pick(parents, group % MICRO), smem_values(row % QUART, group)])
    *attended_own, lse = attend(meta, query, near, far)
    attended_own, lse, ffn_far = together(attended_own, lse, ffn_far)
    attended_parts, grad_ring, ffn_far, ffn_other = together(
        trade_quarter(attended_own), grad_ring, ffn_far, ffn_other
    )
    attended, attn_parts = project(group, attended_parts, attn_full)
    grad_full, grad_t = features(row, grad_ring)

    def both_cores(pieces):
        far_pieces = [(trade(v, "row", 1), apart ^ 1, first) for v, apart, first in pieces]
        return list(pieces) + far_pieces

    pieces = both_cores(
        [(ffn_pack, 0, 0), (ffn_near[0], 2, 0), (ffn_near[1], 6, 0)]
        + [(ffn_far[0], 4, 0), (ffn_far[1], 4, CUT)]
    )
    own_inputs = lax.dynamic_slice_in_dim(inputs, own_start, OWN, 0)
    ffn_full = put_shards(row, None, pieces)
    attn_parts, grad_full, grad_t, ffn_full = together(
        swap(attn_parts, "col"), grad_full, grad_t, ffn_full
    )
    named = routes.reshape(TOK, TOPK, 1) == jnp.arange(EXPERTS, dtype=jnp.int32)
    gate_of = jnp.sum(jnp.where(named, gates.reshape(TOK, TOPK, 1), 0.0), axis=1)
    gate_of = jnp.concatenate(
        [jnp.ones((TOK, 1), F32), gate_of, jnp.zeros((TOK, 15 - EXPERTS), F32)], axis=1
    )
    gate_high = gate_of.astype(BF16)
    gate_low = (gate_of - gate_high.astype(F32)).astype(BF16)
    gate_parts = jnp.concatenate([gate_high, gate_low], axis=1)
    unit = jnp.arange(HID, dtype=jnp.int32)
    expert = jnp.where(unit < SHARED, 0, 1 + (unit - SHARED) // ROUTED)
    spread = (expert[None, :] == jnp.arange(16, dtype=jnp.int32)[:, None]).astype(BF16)
    spread = jnp.concatenate([spread, spread], axis=0)
    attn_parts, gate_parts, spread = together(attn_parts, gate_parts, spread)
    residual, scale_mid, normed_mid = mid(attn_parts, own_inputs, gain_mid)
    normed_mid, other_near = together(normed_mid, near_shards(ffn_other))
    pieces = both_cores([(ffn_other, 8, 0), (other_near[0], 10, 0), (other_near[1], 14, 0)])
    ffn_full = put_shards(row, ffn_full, pieces)
    normed_mid, ffn_full, other_far = together(
        swap(normed_mid, "col"), ffn_full, far_halves(cut_near(other_near))
    )
    normed_mid = normed_mid.reshape(TOK, D)
    pieces = both_cores([(other_far[0], 12, 0), (other_far[1], 12, CUT)])
    ffn_full = put_shards(row, ffn_full, pieces)

    hid, normed_t = hidden(row, normed_mid, grad_full, gate_parts, spread, ffn_full)
    mid_parts = mid_grad(hid, ffn_full)
    hid, normed_t, mid_parts = together(hid, normed_t, mid_parts)
    send = send_grads(1, normed_t, grad_t, hid)
    blocks = keep_grads(1, normed_t, grad_t, hid, trade(send, "row", 1))
    send = send_grads(0, normed_t, grad_t, after(hid, blocks))
    halves = sum_opposite(blocks)
    mid_parts, hid, blocks, send, normed_t = together(
        swap(mid_parts.reshape(COLS, OWN, D), "col"), hid, blocks, send, normed_t
    )
    own_grad = lax.dynamic_slice_in_dim(grad_full, own_start, OWN, 0)
    d_residual, d_low, mid_gain = mid_back(mid_parts, residual, scale_mid, own_grad, gain_mid)
    d_low, hid, send, halves, blocks = together(d_low, hid, send, halves, blocks)
    block, sides = blocks[0], with_opposite(blocks, halves)
    d_low, out_parts, sides, own_blocks = together(
        swap(d_low, "col"),
        output(col, hid, ffn_full, residual),
        sum_neighbours(sides),
        keep_grads(0, normed_t, grad_t, hid, trade(send, "row", 1)),
    )
    other_sum = add_low(block.astype(F32) + sides[0].astype(F32), sides[1])

    d_attended = trade_quarter(project_back(group, d_low, attn_full))
    d_attended, other_sum, out_parts = together(d_attended, other_sum, out_parts)
    *d_query, d_near, d_far = attend_back(
        meta, query, attended_own, d_attended, near, far, lse
    )
    d_query, d_near, d_far, halves, other_low, out_parts, out_left = together(
        d_query,
        d_near,
        d_far,
        sum_opposite(own_blocks),
        trade(other_sum[:CUT], "row", 8),
        out_parts,
        collect_y(out_parts, col // 2, 1),
    )
    d_far = trade(d_far, "row", 1)
    d_query, d_pack = together(trade_quarter(d_query), add_low(d_near, d_far))
    d_query = query_back(group, d_query, cos_wide, sin_wide)
    d_pack, sides, out_right, out_parts, d_query, attn_grads = together(
        swap(d_pack, "row"),
        with_opposite(own_blocks, halves),
        collect_y(out_parts, col // 2, 3),
        out_parts,
        d_query,
        attn_weight_grads(row, normed_in, d_query, d_low.reshape(TOK, D), attended),
    )
    sides = sum_neighbours(sides)

    d_expanded, d_latent, latent_gain = latent_back(
        d_pack, latent_t, cos_t, sin_t, gain_latent, expand_full
    )
    other_high = trade(after(other_sum, d_latent)[CUT:], "row", 8)
    d_latent, attn_grads, out_far, out_own = together(
        swap(d_latent.reshape(COLS, LATC, TOK), "col"),
        add_low(attn_grads[0], trade(attn_grads[1], "row", 1)),
        collect_y(out_parts, col // 2, 2),
        collect_y(out_parts, col // 2, 0),
    )
    out_parts = (out_own, out_left, out_far, out_right)
    d_latent = jnp.sum(d_latent.astype(F32), axis=0).astype(BF16)
    d_latent = jnp.concatenate([d_latent, jnp.zeros((128 - LATC, TOK), BF16)], axis=0).T

    d_tokens, in_gain = input_back(
        col, d_query, d_latent, attn_full, inputs, scale_in, gain_in, d_residual
    )
    d_tokens, in_gain, sides, other_high = together(d_tokens, in_gain, sides, other_high)

    gain = jnp.concatenate([in_gain.reshape(D), latent_gain.reshape(KVL), mid_gain.reshape(D)])
    d_tokens, d_latent = together(d_tokens, d_latent)
    latent_grads = latent_weight_grads(row, normed_in, d_latent, latent_normed_t, d_expanded)
    latent_grads = add_low(latent_grads[0], trade(latent_grads[1], "row", 1))
    ffn_grads = own_blocks[0].astype(F32) + sides[0].astype(F32) + sides[1].astype(F32)
    other_sum = jnp.concatenate([other_low, other_high], axis=0)
    ffn_grads = ffn_grads + other_sum.astype(F32)

    def unpack(at):
        part = ffn_grads[:, at * HID : (at + 1) * HID]
        routed = part[:, SHARED : SHARED + EXPERTS * ROUTED]
        return part[:, :SHARED], routed.reshape(-1, EXPERTS, ROUTED)

    grad_shared_gate, grad_expert_gate = unpack(0)
    grad_shared_up, grad_expert_up = unpack(1)
    grad_shared_down, grad_expert_down = unpack(2)
    ffn_outs = (
        grad_shared_gate,
        grad_shared_up,
        grad_shared_down.T,
        jnp.swapaxes(grad_expert_gate, 0, 1),
        jnp.swapaxes(grad_expert_up, 0, 1),
        grad_expert_down.transpose(1, 2, 0),
    )
    d_tokens, attn_grads, latent_grads, out_parts, gain, ffn_outs = together(
        swap(d_tokens, "col"),
        [reduce_x(attn_grads, j) for j in range(4)],
        latent_grads,
        out_parts,
        gain,
        ffn_outs,
    )
    latent_grads = [reduce_x(latent_grads, j) for j in range(4)]
    attn_grads = reduce_z(attn_grads, latent_grads)
    layer_out = collect_z(out_parts, col % 2).astype(BF16)
    input_grad = jnp.sum(d_tokens.astype(F32), axis=0).astype(BF16)
    gain = share(gain.astype(BF16).reshape(-1, 128), ("row", "col"), ROWS * COLS)
    gain, input_grad, attn_grads, layer_out = together(gain, input_grad, attn_grads, layer_out)
    gain = jnp.sum(gain.astype(F32), axis=0).reshape(-1)
    grad_query = jnp.concatenate(
        [
            attn_grads[:, : heads * NOPE].reshape(-1, heads, NOPE),
            attn_grads[:, heads * NOPE : heads * QK].reshape(-1, heads, ROPE),
        ],
        axis=-1,
    ).reshape(-1, heads * QK)
    grad_output = attn_grads[:, 384:640].T
    grad_expand = attn_grads[:, 640:768].reshape(4, KVL // ROWS, 128)
    grad_expand = grad_expand.transpose(1, 0, 2).reshape(KVL // ROWS, heads * (NOPE + VDIM))
    grad_latent = attn_grads[:, 768 : 768 + LATC]

    return (
        layer_out.reshape(MICRO, BLK, FEAT),
        input_grad.reshape(MICRO, BLK, FEAT),
        gain[:D],
        grad_query,
        grad_latent,
        gain[D : D + KVL],
        grad_expand,
        grad_output,
        gain[D + KVL :],
        *ffn_outs,
    )


def solution(mesh):
    in_specs = (
        P(None, "row", "col"),
        P(None, "row", "col"),
        P(),
        P(None, "row", None),
        P(None, "row", None),
        P(),
        P("row", "col"),
        P("row", "col"),
        P(),
        P("row", "col"),
        P("col", "row"),
        P(),
        P("row", "col"),
        P("row", "col"),
        P("col", "row"),
        P(None, "row", "col"),
        P(None, "row", "col"),
        P(None, "col", "row"),
    )
    out_specs = (
        P(None, "row", "col"),
        P(None, "row", "col"),
        P(),
        P("row", "col"),
        P("row", "col"),
        P(),
        P("row", "col"),
        P("col", "row"),
        P(),
        P("row", "col"),
        P("row", "col"),
        P("col", "row"),
        P(None, "row", "col"),
        P(None, "row", "col"),
        P(None, "col", "row"),
    )
    return jax.shard_map(local, mesh=mesh, in_specs=in_specs, out_specs=out_specs, check_vma=False)
```

profile of v0, /device:TPU:0, one launch (start us, length us, event | category | flops | bytes accessed | tf_op | source)
XLA Modules:
  0.0 576.5 jit_solution(6359115889675097906)
XLA Ops:
  34.6 8.1 %collective-permute-done.2 = bf16[2,128,896]{2,1,0:T(8,128)(2,1)S(1)} collective-permute-done((bf16[2,128,896]{2,1,0:T(8,128)(2,1)S(1)}, bf16[2,128,896]{2,1,0:T(8,128)(2,1)S(1)}, u32[]{:S(2)}, u32[]{:S(2)}) %collective-permute-start.2) | collective-permute-done | bytes 458784 | tf_op jit(solution)/shard_map/ppermute | solution.py:82
  42.7 9.5 %collective-permute-done.3 = bf16[2,128,896]{2,1,0:T(8,128)(2,1)S(1)} collective-permute-done((bf16[2,128,896]{2,1,0:T(8,128)(2,1)S(1)}, bf16[2,128,896]{2,1,0:T(8,128)(2,1)S(1)}, u32[]{:S(2)}, u32[]{:S(2)}) %collective-permute-start.3) | collective-permute-done | bytes 458784 | tf_op jit(solution)/shard_map/ppermute | solution.py:82
  112.0 16.2 %collective-permute-done.9.q1.refs_1_ = bf16[256,256]{1,0:T(8,128)(2,1)S(1)} collective-permute-done((bf16[256,256]{1,0:T(8,128)(2,1)S(1)}, bf16[256,256]{1,0:T(8,128)(2,1)S(1)}, u32[]{:S(2)}, u32[]{:S(2)}) %collective-permute-start.9) | collective-permute-done | bytes 131104 | tf_op jit(solution)/shard_map/ppermute | solution.py:82
  143.7 10.2 %shard_map.294 = (bf16[256,128]{1,0:T(8,128)(2,1)}, bf16[256,128]{1,0:T(8,128)(2,1)}, bf16[256,128]{1,0:T(8,128)(2,1)}, bf16[256,128]{1,0:T(8,128)(2,1)}, f32[4,1,256]{2,1,0:T(1,128)}) custom-call(s32[15]{0:T(128)} %pad_add_fusion.meta, bf16[256,256]{1,0:T(8,128)(2,1)} %get-tuple-element.270.q0.refs_0_, bf16[256,256]{1,0:T(8,128)(2,1)} %copy-done.50, ...), custom_call_target="tpu_custom_call" | custom-call | flops 1342177280 | bytes 4194304 | tf_op jit(solution)/shard_map/pallas_call | solution.py:416
  191.7 8.3 %shard_map.297.refs_6_ = bf16[2048,5376]{1,0:T(8,128)(2,1)} custom-call(s32[1]{0:T(128)} %bitcast.26.own_ref, bf16[128,5376]{1,0:T(8,128)(2,1)} %concatenate.39.refs_0_, bf16[128,5376]{1,0:T(8,128)(2,1)} %collective-permute-done.7.refs_1_, bf16[128,5376]{1,0:T(8,128)(2,1)} %copy-done.18, bf16[64,5376]{1,0:T(8,128)(2,1)} %collective-permute-done.13.refs_3_, ...), custom_call_target="tpu_custom_call" | custom-call | bytes 1048576 | tf_op jit(solution)/shard_map/pallas_call | solution.py:191
  199.9 8.6 %all-to-all-done.4.parts_ref = bf16[8,64,2048]{2,1,0:T(8,128)(2,1)S(1)} async-done(((bf16[8,64,2048]{2,1,0:T(8,128)(2,1)}), bf16[8,64,2048]{2,1,0:T(8,128)(2,1)S(1)}, u32[]{:S(2)}, u32[]{:S(2)}) %all-to-all-start.4) | async-done | bytes 2097184 | tf_op jit(solution)/shard_map/all_to_all | solution.py:73
  229.3 6.6 %shard_map.299.refs_4_ = bf16[2048,5376]{1,0:T(8,128)(2,1)} custom-call(s32[1]{0:T(128)} %bitcast.26.own_ref, bf16[128,5376]{1,0:T(8,128)(2,1)} %collective-permute-done.5.refs_0_, bf16[128,5376]{1,0:T(8,128)(2,1)} %collective-permute-done.23.refs_1_, bf16[128,5376]{1,0:T(8,128)(2,1)} %collective-permute-done.24.refs_2_, ...), custom_call_target="tpu_custom_call", output_to_operand_aliasing={{}: (7, {})} | custom-call | bytes 1048576 | tf_op jit(solution)/shard_map/pallas_call | solution.py:191
  235.9 8.5 %collective-permute-done.28.refs_0_ = bf16[64,5376]{1,0:T(8,128)(2,1)S(1)} collective-permute-done((bf16[64,5376]{1,0:T(8,128)(2,1)}, bf16[64,5376]{1,0:T(8,128)(2,1)S(1)}, u32[]{:S(2)}, u32[]{:S(2)}) %collective-permute-start.28) | collective-permute-done | bytes 688160 | tf_op jit(solution)/shard_map/ppermute | solution.py:82
  258.8 19.9 %shard_map.301 = (bf16[3,512,1792]{2,1,0:T(8,128)(2,1)}, bf16[2048,512]{1,0:T(8,128)(2,1)}) custom-call(s32[1]{0:T(128)} %bitcast.26.own_ref, bf16[512,2048]{1,0:T(8,128)(2,1)} %bitcast.147, bf16[512,2048]{1,0:T(8,128)(2,1)} %get-tuple-element.310.grad_ref, bf16[512,32]{1,0:T(8,128)(2,1)} %copy.173.gate_ref, bf16[32,1792]{1,0:T(8,128)(2,1)} %add_convert_fusion.7.spread_ref, ...), custom_call_target="tpu_custom_call" | custom-call | flops 11274289152 | bytes 33554432 | tf_op jit(solution)/shard_map/pallas_call | solution.py:816
  278.7 12.6 %shard_map.302 = bf16[512,2048]{1,0:T(8,128)(2,1)} custom-call(bf16[3,512,1792]{2,1,0:T(8,128)(2,1)} %get-tuple-element.338.hid_ref, bf16[2048,5376]{1,0:T(8,128)(2,1)} %shard_map.300.wg_ref.wu_ref.wd_ref.w_ref), custom_call_target="tpu_custom_call" | custom-call | flops 7516192768 | bytes 20971520 | tf_op jit(solution)/shard_map/pallas_call | solution.py:850
  291.3 7.6 %shard_map.303 = bf16[512,5376]{1,0:T(8,128)(2,1)} custom-call(bf16[2048,512]{1,0:T(8,128)(2,1)} %get-tuple-element.345.mid_ref, bf16[2048,512]{1,0:T(8,128)(2,1)} %get-tuple-element.321.grad_ref, bf16[3,512,1792]{2,1,0:T(8,128)(2,1)} %get-tuple-element.338.hid_ref), custom_call_target="tpu_custom_call" | custom-call | flops 58720256 | bytes 1048576 | tf_op jit(solution)/shard_map/pallas_call | solution.py:1048
  308.3 9.2 %shard_map.304 = (bf16[128,5376]{1,0:T(8,128)(2,1)}, bf16[128,5376]{1,0:T(8,128)(2,1)}, bf16[64,5376]{1,0:T(8,128)(2,1)}, bf16[64,5376]{1,0:T(8,128)(2,1)}, bf16[128,5376]{1,0:T(8,128)(2,1)}) custom-call(bf16[2048,512]{1,0:T(8,128)(2,1)} %get-tuple-element.345.mid_ref, bf16[2048,512]{1,0:T(8,128)(2,1)} %get-tuple-element.321.grad_ref, ...), custom_call_target="tpu_custom_call" | custom-call | flops 58720256 | bytes 1048576 | tf_op jit(solution)/shard_map/pallas_call | solution.py:1065
  320.2 7.7 %shard_map.305 = bf16[512,5376]{1,0:T(8,128)(2,1)} custom-call(bf16[2048,512]{1,0:T(8,128)(2,1)} %get-tuple-element.345.mid_ref, bf16[2048,512]{1,0:T(8,128)(2,1)} %get-tuple-element.321.grad_ref, bf16[3,512,1792]{2,1,0:T(8,128)(2,1)} %get-tuple-element.338.hid_ref), custom_call_target="tpu_custom_call" | custom-call | flops 58720256 | bytes 1048576 | tf_op jit(solution)/shard_map/pallas_call | solution.py:1048
  327.9 6.9 %all-to-all-done.6.parts_ref = bf16[8,64,2048]{2,1,0:T(8,128)(2,1)S(1)} async-done(((bf16[8,64,2048]{2,1,0:T(8,128)(2,1)}), bf16[8,64,2048]{2,1,0:T(8,128)(2,1)S(1)}, u32[]{:S(2)}, u32[]{:S(2)}) %all-to-all-start.6) | async-done | bytes 2097184 | tf_op jit(solution)/shard_map/all_to_all | solution.py:73
  347.1 11.2 %shard_map.307 = bf16[8,512,256]{2,1,0:T(8,128)(2,1)} custom-call(s32[1]{0:T(128)} %bitcast.col_ref, bf16[3,512,1792]{2,1,0:T(8,128)(2,1)} %get-tuple-element.338.hid_ref, bf16[2048,5376]{1,0:T(8,128)(2,1)} %shard_map.300.wg_ref.wu_ref.wd_ref.w_ref, f32[64,2048]{1,0:T(8,128)} %copy-done.6), custom_call_target="tpu_custom_call" | custom-call | flops 234881024 | bytes 1048576 | tf_op jit(solution)/shard_map/pallas_call | solution.py:875
  358.2 9.2 %shard_map.309 = (bf16[128,5376]{1,0:T(8,128)(2,1)}, bf16[128,5376]{1,0:T(8,128)(2,1)}, bf16[64,5376]{1,0:T(8,128)(2,1)}, bf16[64,5376]{1,0:T(8,128)(2,1)}, bf16[128,5376]{1,0:T(8,128)(2,1)}) custom-call(bf16[2048,512]{1,0:T(8,128)(2,1)} %get-tuple-element.345.mid_ref, bf16[2048,512]{1,0:T(8,128)(2,1)} %get-tuple-element.321.grad_ref, ...), custom_call_target="tpu_custom_call" | custom-call | flops 58720256 | bytes 1048576 | tf_op jit(solution)/shard_map/pallas_call | solution.py:1065
  367.4 10.6 %collective-permute-done.35 = bf16[128,5376]{1,0:T(8,128)(2,1)S(1)} collective-permute-done((bf16[128,5376]{1,0:T(8,128)(2,1)}, bf16[128,5376]{1,0:T(8,128)(2,1)S(1)}, u32[]{:S(2)}, u32[]{:S(2)}) %collective-permute-start.35) | collective-permute-done | bytes 1376288 | tf_op jit(solution)/shard_map/ppermute | solution.py:82
  403.2 12.3 %shard_map.311 = (bf16[256,256]{1,0:T(8,128)(2,1)}, bf16[256,256]{1,0:T(8,128)(2,1)}, bf16[256,256]{1,0:T(8,128)(2,1)}, bf16[256,256]{1,0:T(8,128)(2,1)}, bf16[1...) custom-call(s32[15]{0:T(128)} %pad_add_fusion.meta, bf16[256,256]{1,0:T(8,128)(2,1)} %get-tuple-element.270.q0.refs_0_, ...), custom_call_target="tpu_custom_call" | custom-call | flops 3489660928 | bytes 10485760 | tf_op jit(solution)/shard_map/pallas_call | solution.py:500
  443.8 8.1 %shard_map.314 = (bf16[8,128,640]{2,1,0:T(8,128)(2,1)}, bf16[8,128,640]{2,1,0:T(8,128)(2,1)}) custom-call(s32[1]{0:T(128)} %bitcast.26.own_ref, bf16[512,2048]{1,0:T(8,128)(2,1)} %get-tuple-element.394.normed_ref.x_ref, bf16[512,384]{1,0:T(8,128)(2,1)} %shard_map.313.dq_ref, bf16[512,2048]{1,0:T(8,128)(2,1)} %bitcast.145, ...), custom_call_target="tpu_custom_call" | custom-call | flops 16777216 | bytes 1048576 | tf_op jit(solution)/shard_map/pallas_call | solution.py:275
  451.8 7.1 %all-to-all-done.8.pack_ref = bf16[16,128,384]{2,1,0:T(8,128)(2,1)} async-done(((bf16[16,128,384]{2,1,0:T(8,128)(2,1)}), bf16[16,128,384]{2,1,0:T(8,128)(2,1)}, u32[]{:S(2)}, u32[]{:S(2)}) %all-to-all-start.8) | async-done | bytes 1572896 | tf_op jit(solution)/shard_map/all_to_all | solution.py:73
  488.8 8.0 %shard_map.316 = (bf16[8,512,256]{2,1,0:T(8,128)(2,1)}, f32[1,2048]{1,0:T(1,128)}) custom-call(s32[1]{0:T(128)} %bitcast.col_ref, bf16[512,384]{1,0:T(8,128)(2,1)} %shard_map.313.dq_ref, bf16[512,128]{1,0:T(8,128)(2,1)} %pad_bitcast_fusion.dl_ref, bf16[2048,896]{1,0:T(8,128)(2,1)} %bitcast.136, bf16[2048,896]{1,0:T(8,128)(2,1)} %bitcast.137, ...), custom_call_target="tpu_custom_call" | custom-call | flops 1342177280 | bytes 9437184 | tf_op jit(solution)/shard_map/pallas_call | solution.py:978
  502.6 7.0 %shard_map.317 = (bf16[8,128,256]{2,1,0:T(8,128)(2,1)}, bf16[8,128,256]{2,1,0:T(8,128)(2,1)}) custom-call(s32[1]{0:T(128)} %bitcast.26.own_ref, bf16[512,2048]{1,0:T(8,128)(2,1)} %get-tuple-element.394.normed_ref.x_ref, bf16[512,128]{1,0:T(8,128)(2,1)} %pad_bitcast_fusion.dl_ref, bf16[512,512]{1,0:T(8,128)(2,1)} %copy-done.12, ...), custom_call_target="tpu_custom_call" | custom-call | flops 16777216 | bytes 1048576 | tf_op jit(solution)/shard_map/pallas_call | solution.py:275
  522.3 10.6 %all-to-all-done.10 = bf16[8,512,256]{2,1,0:T(8,128)(2,1)} async-done(((bf16[8,512,256]{2,1,0:T(8,128)(2,1)}), bf16[8,512,256]{2,1,0:T(8,128)(2,1)}, u32[]{:S(2)}, u32[]{:S(2)}) %all-to-all-start.10) | async-done | bytes 2097184 | tf_op jit(solution)/shard_map/all_to_all | solution.py:73
  554.0 7.2 %collective-permute-done.61 = bf16[2,128,256]{2,1,0:T(8,128)(2,1)} collective-permute-done((bf16[2,128,256]{2,1,0:T(8,128)(2,1)}, bf16[2,128,256]{2,1,0:T(8,128)(2,1)}, u32[]{:S(2)}, u32[]{:S(2)}) %collective-permute-start.61) | collective-permute-done | bytes 131104 | tf_op jit(solution)/shard_map/ppermute | solution.py:82
  (377 shorter events, 343.3 us)
Async XLA Ops:
  21.5 37.1 %all-to-all-start = ((bf16[4,2,512,256]{3,2,1,0:T(8,128)(2,1)}), bf16[4,2,512,256]{3,2,1,0:T(8,128)(2,1)S(1)}, u32[]{:S(2)}, u32[]{:S(2)}) async-start(bf16[4,2,512,256]{3,2,1,0:T(8,128)(2,1)} %broadcast_in_dim.60), calls=%async_computation | async-start | bytes 4194304 | tf_op jit(solution)/shard_map/all_to_all | solution.py:73
  25.9 32.6 %collective-permute-start.5 = (bf16[128,5376]{1,0:T(8,128)(2,1)}, bf16[128,5376]{1,0:T(8,128)(2,1)}, u32[]{:S(2)}, u32[]{:S(2)}) collective-permute-start(bf16[128,5376]{1,0:T(8,128)(2,1)} %concatenate.39.refs_0_), channel_id=1, source_target_pairs={{0,64},{8,72},{16,80},{24,88},{32,96},{40,104},{48,112},{56,120},{... | collective-permute-start | bytes 4128776 | tf_op jit(solution)/shard_map/ppermute | solution.py:82
  61.6 32.9 %collective-permute-start.7 = (bf16[128,5376]{1,0:T(8,128)(2,1)}, bf16[128,5376]{1,0:T(8,128)(2,1)}, u32[]{:S(2)}, u32[]{:S(2)}) collective-permute-start(bf16[128,5376]{1,0:T(8,128)(2,1)} %concatenate.39.refs_0_), channel_id=1, source_target_pairs={{0,16},{8,24},{16,0},{24,8},{32,48},{40,56},{48,32},{56,40},{64,80... | collective-permute-start | bytes 4128776 | tf_op jit(solution)/shard_map/ppermute | solution.py:82
  63.1 33.7 %collective-permute-start.8 = (bf16[128,5376]{1,0:T(8,128)(2,1)}, bf16[128,5376]{1,0:T(8,128)(2,1)S(1)}, u32[]{:S(2)}, u32[]{:S(2)}) collective-permute-start(bf16[128,5376]{1,0:T(8,128)(2,1)} %concatenate.39.refs_0_), channel_id=1, source_target_pairs={{0,48},{8,56},{16,32},{24,40},{32,16},{40,24},{48,0},{56,8},{64,11... | collective-permute-start | bytes 4128776 | tf_op jit(solution)/shard_map/ppermute | solution.py:82
  98.8 34.2 %all-to-all-start.2 = ((bf16[16,128,384]{2,1,0:T(8,128)(2,1)}), bf16[16,128,384]{2,1,0:T(8,128)(2,1)}, u32[]{:S(2)}, u32[]{:S(2)}) async-start(bf16[16,128,384]{2,1,0:T(8,128)(2,1)} %get-tuple-element.262), calls=%async_computation.2 | async-start | bytes 3145728 | tf_op jit(solution)/shard_map/all_to_all | solution.py:73
  134.5 36.3 %all-to-all-start.3 = ((bf16[8,512,256]{2,1,0:T(8,128)(2,1)}), bf16[8,512,256]{2,1,0:T(8,128)(2,1)S(1)}, u32[]{:S(2)}, u32[]{:S(2)}) async-start(bf16[8,512,256]{2,1,0:T(8,128)(2,1)} %broadcast_in_dim.63), calls=%async_computation.3 | async-start | bytes 4194304 | tf_op jit(solution)/shard_map/all_to_all | solution.py:73
  142.3 41.9 %collective-permute-start.18 = (bf16[128,5376]{1,0:T(8,128)(2,1)}, bf16[128,5376]{1,0:T(8,128)(2,1)}, u32[]{:S(2)}, u32[]{:S(2)}) collective-permute-start(bf16[128,5376]{1,0:T(8,128)(2,1)} %concatenate.39.refs_0_), channel_id=1, source_target_pairs={{0,8},{8,0},{16,24},{24,16},{32,40},{40,32},{48,56},{56,48},{64,72... | collective-permute-start | bytes 4128776 | tf_op jit(solution)/shard_map/ppermute | solution.py:82
  142.6 41.7 %collective-permute-start.19 = (bf16[128,5376]{1,0:T(8,128)(2,1)}, bf16[128,5376]{1,0:T(8,128)(2,1)}, u32[]{:S(2)}, u32[]{:S(2)}) collective-permute-start(bf16[128,5376]{1,0:T(8,128)(2,1)} %collective-permute-done.7.refs_1_), channel_id=1, source_target_pairs={{0,8},{8,0},{16,24},{24,16},{32,40},{40,32},{48,56},{56,48},{64,72... | collective-permute-start | bytes 4128776 | tf_op jit(solution)/shard_map/ppermute | solution.py:82
  175.7 32.8 %all-to-all-start.4 = ((bf16[8,64,2048]{2,1,0:T(8,128)(2,1)}), bf16[8,64,2048]{2,1,0:T(8,128)(2,1)S(1)}, u32[]{:S(2)}, u32[]{:S(2)}) async-start(bf16[8,64,2048]{2,1,0:T(8,128)(2,1)} %get-tuple-element.294), calls=%async_computation.4 | async-start | bytes 4194304 | tf_op jit(solution)/shard_map/all_to_all | solution.py:73
  181.2 32.9 %collective-permute-start.23 = (bf16[128,5376]{1,0:T(8,128)(2,1)}, bf16[128,5376]{1,0:T(8,128)(2,1)}, u32[]{:S(2)}, u32[]{:S(2)}) collective-permute-start(bf16[128,5376]{1,0:T(8,128)(2,1)} %collective-permute-done.5.refs_0_), channel_id=1, source_target_pairs={{0,16},{8,24},{16,0},{24,8},{32,48},{40,56},{48,32},{56,40},{64,80... | collective-permute-start | bytes 4128776 | tf_op jit(solution)/shard_map/ppermute | solution.py:82
  182.4 33.8 %collective-permute-start.24 = (bf16[128,5376]{1,0:T(8,128)(2,1)}, bf16[128,5376]{1,0:T(8,128)(2,1)}, u32[]{:S(2)}, u32[]{:S(2)}) collective-permute-start(bf16[128,5376]{1,0:T(8,128)(2,1)} %collective-permute-done.5.refs_0_), channel_id=1, source_target_pairs={{0,48},{8,56},{16,32},{24,40},{32,16},{40,24},{48,0},{56,8},{64,11... | collective-permute-start | bytes 4128776 | tf_op jit(solution)/shard_map/ppermute | solution.py:82
  216.2 35.9 %all-to-all-start.5 = ((bf16[8,64,2048]{2,1,0:T(8,128)(2,1)}), bf16[8,64,2048]{2,1,0:T(8,128)(2,1)S(1)}, u32[]{:S(2)}, u32[]{:S(2)}) async-start(bf16[8,64,2048]{2,1,0:T(8,128)(2,1)} %copy-done.8), calls=%async_computation.5 | async-start | bytes 4194304 | tf_op jit(solution)/shard_map/all_to_all | solution.py:73
  299.0 35.8 %all-to-all-start.6 = ((bf16[8,64,2048]{2,1,0:T(8,128)(2,1)}), bf16[8,64,2048]{2,1,0:T(8,128)(2,1)S(1)}, u32[]{:S(2)}, u32[]{:S(2)}) async-start(bf16[8,64,2048]{2,1,0:T(8,128)(2,1)} %bitcast.146), calls=%async_computation.6 | async-start | bytes 4194304 | tf_op jit(solution)/shard_map/all_to_all | solution.py:73
  337.7 41.8 %all-to-all-start.7 = ((bf16[8,64,2048]{2,1,0:T(8,128)(2,1)}), bf16[8,64,2048]{2,1,0:T(8,128)(2,1)S(1)}, u32[]{:S(2)}, u32[]{:S(2)}) async-start(bf16[8,64,2048]{2,1,0:T(8,128)(2,1)} %copy-done.7), calls=%async_computation.7 | async-start | bytes 4194304 | tf_op jit(solution)/shard_map/all_to_all | solution.py:73
  345.2 32.8 %collective-permute-start.35 = (bf16[128,5376]{1,0:T(8,128)(2,1)}, bf16[128,5376]{1,0:T(8,128)(2,1)S(1)}, u32[]{:S(2)}, u32[]{:S(2)}) collective-permute-start(bf16[128,5376]{1,0:T(8,128)(2,1)} %get-tuple-element.343), channel_id=1, source_target_pairs={{0,16},{8,24},{16,0},{24,8},{32,48},{40,56},{48,32},{56,40},{64,80... | collective-permute-start | bytes 4128776 | tf_op jit(solution)/shard_map/ppermute | solution.py:82
  345.2 34.3 %collective-permute-start.36 = (bf16[128,5376]{1,0:T(8,128)(2,1)}, bf16[128,5376]{1,0:T(8,128)(2,1)}, u32[]{:S(2)}, u32[]{:S(2)}) collective-permute-start(bf16[128,5376]{1,0:T(8,128)(2,1)} %get-tuple-element.344), channel_id=1, source_target_pairs={{0,48},{8,56},{16,32},{24,40},{32,16},{40,24},{48,0},{56,8},{64,11... | collective-permute-start | bytes 4128776 | tf_op jit(solution)/shard_map/ppermute | solution.py:82
  429.4 29.6 %all-to-all-start.8 = ((bf16[16,128,384]{2,1,0:T(8,128)(2,1)}), bf16[16,128,384]{2,1,0:T(8,128)(2,1)}, u32[]{:S(2)}, u32[]{:S(2)}) async-start(bf16[16,128,384]{2,1,0:T(8,128)(2,1)} %add_convert_fusion), calls=%async_computation.8 | async-start | bytes 3145728 | tf_op jit(solution)/shard_map/all_to_all | solution.py:73
  459.0 38.7 %collective-permute-start.52 = (bf16[128,5376]{1,0:T(8,128)(2,1)}, bf16[128,5376]{1,0:T(8,128)(2,1)}, u32[]{:S(2)}, u32[]{:S(2)}) collective-permute-start(bf16[128,5376]{1,0:T(8,128)(2,1)} %get-tuple-element.409), channel_id=1, source_target_pairs={{0,16},{8,24},{16,0},{24,8},{32,48},{40,56},{48,32},{56,40},{64,80... | collective-permute-start | bytes 4128776 | tf_op jit(solution)/shard_map/ppermute | solution.py:82
  459.0 38.7 %collective-permute-start.53 = (bf16[128,5376]{1,0:T(8,128)(2,1)}, bf16[128,5376]{1,0:T(8,128)(2,1)}, u32[]{:S(2)}, u32[]{:S(2)}) collective-permute-start(bf16[128,5376]{1,0:T(8,128)(2,1)} %get-tuple-element.410), channel_id=1, source_target_pairs={{0,48},{8,56},{16,32},{24,40},{32,16},{40,24},{48,0},{56,8},{64,11... | collective-permute-start | bytes 4128776 | tf_op jit(solution)/shard_map/ppermute | solution.py:82
  484.1 38.2 %collective-permute-start.55 = (bf16[2,128,640]{2,1,0:T(8,128)(2,1)}, bf16[2,128,640]{2,1,0:T(8,128)(2,1)}, u32[]{:S(2)}, u32[]{:S(2)}) collective-permute-start(bf16[2,128,640]{2,1,0:T(8,128)(2,1)} %get-tuple-element.538), channel_id=1, source_target_pairs={{0,16},{8,24},{16,0},{24,8},{32,48},{40,56},{48,32},{56,40},{64,80... | collective-permute-start | bytes 983048 | tf_op jit(solution)/shard_map/ppermute | solution.py:82
  485.5 36.9 %collective-permute-start.56 = (bf16[2,128,640]{2,1,0:T(8,128)(2,1)}, bf16[2,128,640]{2,1,0:T(8,128)(2,1)}, u32[]{:S(2)}, u32[]{:S(2)}) collective-permute-start(bf16[2,128,640]{2,1,0:T(8,128)(2,1)} %get-tuple-element.537), channel_id=1, source_target_pairs={{0,32},{8,40},{16,48},{24,56},{32,0},{40,8},{48,16},{56,24},{64,96... | collective-permute-start | bytes 983048 | tf_op jit(solution)/shard_map/ppermute | solution.py:82
  496.8 25.5 %collective-permute-start.57 = (bf16[2,128,640]{2,1,0:T(8,128)(2,1)}, bf16[2,128,640]{2,1,0:T(8,128)(2,1)}, u32[]{:S(2)}, u32[]{:S(2)}) collective-permute-start(bf16[2,128,640]{2,1,0:T(8,128)(2,1)} %get-tuple-element.536), channel_id=1, source_target_pairs={{0,48},{8,56},{16,32},{24,40},{32,16},{40,24},{48,0},{56,8},{64,11... | collective-permute-start | bytes 983048 | tf_op jit(solution)/shard_map/ppermute | solution.py:82
  497.7 35.3 %all-to-all-start.10 = ((bf16[8,512,256]{2,1,0:T(8,128)(2,1)}), bf16[8,512,256]{2,1,0:T(8,128)(2,1)}, u32[]{:S(2)}, u32[]{:S(2)}) async-start(bf16[8,512,256]{2,1,0:T(8,128)(2,1)} %get-tuple-element.413), calls=%async_computation.10 | async-start | bytes 4194304 | tf_op jit(solution)/shard_map/all_to_all | solution.py:73
  534.2 37.2 %all-to-all-start.11 = ((bf16[128,36,128]{2,1,0:T(8,128)(2,1)}), bf16[128,36,128]{2,1,0:T(8,128)(2,1)S(1)}, u32[]{:S(2)}, u32[]{:S(2)}) async-start(bf16[128,36,128]{2,1,0:T(8,128)(2,1)} %broadcast_in_dim.71), calls=%async_computation.11 | async-start | bytes 2621440 | tf_op jit(solution)/shard_map/all_to_all | solution.py:73
  (108 other events, 1322.1 us)
where the time goes:
time: 587 us; the launch traced here: 577 us
  Pallas kernels  184 us (31%)
  waiting for transfers between devices  168 us (29%)
  starting transfers between devices  138 us (24%)
  local copies, waits for them, and re-layouts  58.5 us (10%)
  other arithmetic  26.1 us (4%)
    ppermute x64, waiting for transfers between devices, trade(): return lax.ppermute(values, axis, [(i, i ^ mask) for i in range(count)])  122 us
    ppermute x64, starting transfers between devices, trade(): return lax.ppermute(values, axis, [(i, i ^ mask) for i in range(count)])  81.3 us
    all_to_all x12, starting transfers between devices, swap(): lax.all_to_all(values, axis, 0, 0, tiled=True, axis_index_groups=groups)  56.5 us
    all_to_all x12, waiting for transfers between devices, swap(): lax.all_to_all(values, axis, 0, 0, tiled=True, axis_index_groups=groups)  45.8 us
    unnamed x128, local copies, waits for them, and re-layouts  20.1 us
    pallas_call x1, Pallas kernels, hidden(): pl.pallas_call(hidden_kernel, grid=(parts,), out_shape=(jax.ShapeDtypeStr...  19.9 us
    pallas_call x2, Pallas kernels, keep_grads(): pl.pallas_call(keep_grad_kernel, grid=(3,), out_shape=[jax.ShapeDtypeStru...  18.5 us
    pallas_call x3, Pallas kernels, put_shards(): pl.pallas_call(functools.partial(put_kernel, places), out_shape=jax.Shape...  18.2 us
  transfers between devices with their start and end apart: 76, of which 35 were waited for; matrix products, arithmetic and copies ran while one was open for 10% of the time, Pallas kernels for 23%

commit v1 on v0

--- a/solution.py
+++ b/solution.py
@@ -1173,19 +1173,18 @@
 
     inputs, normed_in, scale_in, latent_parts = front(col, input_ring, gain_in, attn_full)
     query = project_query(group, normed_in, attn_full, cos_wide, sin_wide)
-    latent_t, query, normed_in, ffn_near = together(
-        swap(latent_parts, "col"), query, normed_in, ffn_near
+    latent_t, query, normed_in, ffn_near, grad_copies = together(
+        swap(latent_parts, "col"),
+        query,
+        normed_in,
+        ffn_near,
+        jnp.broadcast_to(out_grad.reshape(1, TOK, FEAT), (COLS, TOK, FEAT)),
     )
     latent_t = latent_t.reshape(LAT, TOK)
     latent_normed_t, pack = expand(latent_t, cos_t, sin_t, gain_latent, expand_full)
-    pack, query, ffn_near, out_grad, ffn_other = together(
-        pack, query, ffn_near, out_grad, ffn_other
-    )
+    pack, query, ffn_near, ffn_other = together(pack, query, ffn_near, ffn_other)
     near, query, ffn_cut, grad_copies = together(
-        swap(pack, "row"),
-        trade_quarter(query),
-        cut_near(ffn_near),
-        jnp.broadcast_to(out_grad.reshape(1, TOK, FEAT), (COLS, TOK, FEAT)),
+        swap(pack, "row"), trade_quarter(query), cut_near(ffn_near), grad_copies
     )
     grad_ring = swap(grad_copies, "col")
     ffn_far = far_halves(ffn_cut)

time: 587 us -> 587 us (level)
    unnamed x128 -> x122, local copies, waits for them, and re-layouts: 20.1 us -> 20.1 us
  transfers between devices with their start and end apart: 76 -> 76, of which waited for: 35 -> 36; matrix products, arithmetic and copies ran while one was open for 10% -> 10% of each run, Pallas kernels for 23% -> 23%
where the time goes in v1:
time: 587 us; the launch traced here: 576 us
  Pallas kernels  179 us (30%)
  waiting for transfers between devices  172 us (29%)
  starting transfers between devices  138 us (24%)
  local copies, waits for them, and re-layouts  58.6 us (10%)
  other arithmetic  26.1 us (4%)
    ppermute x64, waiting for transfers between devices, trade(): return lax.ppermute(values, axis, [(i, i ^ mask) for i in range(count)])  127 us
    ppermute x64, starting transfers between devices, trade(): return lax.ppermute(values, axis, [(i, i ^ mask) for i in range(count)])  82.4 us
    all_to_all x12, starting transfers between devices, swap(): lax.all_to_all(values, axis, 0, 0, tiled=True, axis_index_groups=groups)  55.3 us
    all_to_all x12, waiting for transfers between devices, swap(): lax.all_to_all(values, axis, 0, 0, tiled=True, axis_index_groups=groups)  45.1 us
    unnamed x122, local copies, waits for them, and re-layouts  20.1 us
    pallas_call x1, Pallas kernels, hidden(): pl.pallas_call(hidden_kernel, grid=(parts,), out_shape=(jax.ShapeDtypeStr...  19.9 us
    pallas_call x2, Pallas kernels, keep_grads(): pl.pallas_call(keep_grad_kernel, grid=(3,), out_shape=[jax.ShapeDtypeStru...  18.4 us
    pallas_call x3, Pallas kernels, put_shards(): pl.pallas_call(functools.partial(put_kernel, places), out_shape=jax.Shape...  18.2 us
  transfers between devices with their start and end apart: 76, of which 36 were waited for; matrix products, arithmetic and copies ran while one was open for 10% of the time, Pallas kernels for 23%

profile of v1, /device:TPU:0, one launch (start us, length us, event | category | flops | bytes accessed | tf_op | source)
XLA Modules:
  0.0 575.6 jit_solution(13779865285072465265)
XLA Ops:
  34.6 8.1 %collective-permute-done.2 = bf16[2,128,896]{2,1,0:T(8,128)(2,1)S(1)} collective-permute-done((bf16[2,128,896]{2,1,0:T(8,128)(2,1)S(1)}, bf16[2,128,896]{2,1,0:T(8,128)(2,1)S(1)}, u32[]{:S(2)}, u32[]{:S(2)}) %collective-permute-start.2) | collective-permute-done | bytes 458784 | tf_op jit(solution)/shard_map/ppermute | solution.py:82
  42.7 9.5 %collective-permute-done.3 = bf16[2,128,896]{2,1,0:T(8,128)(2,1)S(1)} collective-permute-done((bf16[2,128,896]{2,1,0:T(8,128)(2,1)S(1)}, bf16[2,128,896]{2,1,0:T(8,128)(2,1)S(1)}, u32[]{:S(2)}, u32[]{:S(2)}) %collective-permute-start.3) | collective-permute-done | bytes 458784 | tf_op jit(solution)/shard_map/ppermute | solution.py:82
  113.5 16.3 %collective-permute-done.9.q1.refs_1_ = bf16[256,256]{1,0:T(8,128)(2,1)} collective-permute-done((bf16[256,256]{1,0:T(8,128)(2,1)S(1)}, bf16[256,256]{1,0:T(8,128)(2,1)}, u32[]{:S(2)}, u32[]{:S(2)}) %collective-permute-start.9) | collective-permute-done | bytes 131104 | tf_op jit(solution)/shard_map/ppermute | solution.py:82
  143.8 7.8 %shard_map.294 = (bf16[256,128]{1,0:T(8,128)(2,1)}, bf16[256,128]{1,0:T(8,128)(2,1)}, bf16[256,128]{1,0:T(8,128)(2,1)}, bf16[256,128]{1,0:T(8,128)(2,1)}, f32[4,1,256]{2,1,0:T(1,128)}) custom-call(s32[15]{0:T(128)} %pad_add_fusion.meta, bf16[256,256]{1,0:T(8,128)(2,1)} %get-tuple-element.270.q0.refs_0_, bf16[256,256]{1,0:T(8,128)(2,1)} %collective-permute-done.9.q1.refs_1_, ...), custom_call_target="tpu_custom_call" | custom-call | flops 1342177280 | bytes 4194304 | tf_op jit(solution)/shard_map/pallas_call | solution.py:416
  191.7 8.2 %shard_map.297.refs_6_ = bf16[2048,5376]{1,0:T(8,128)(2,1)} custom-call(s32[1]{0:T(128)} %bitcast.26.own_ref, bf16[128,5376]{1,0:T(8,128)(2,1)} %concatenate.39.refs_0_, bf16[128,5376]{1,0:T(8,128)(2,1)} %collective-permute-done.7.refs_1_, bf16[128,5376]{1,0:T(8,128)(2,1)} %copy-done.18, bf16[64,5376]{1,0:T(8,128)(2,1)} %collective-permute-done.13.refs_3_, ...), custom_call_target="tpu_custom_call" | custom-call | bytes 1048576 | tf_op jit(solution)/shard_map/pallas_call | solution.py:191
  200.0 8.6 %all-to-all-done.4.parts_ref = bf16[8,64,2048]{2,1,0:T(8,128)(2,1)S(1)} async-done(((bf16[8,64,2048]{2,1,0:T(8,128)(2,1)}), bf16[8,64,2048]{2,1,0:T(8,128)(2,1)S(1)}, u32[]{:S(2)}, u32[]{:S(2)}) %all-to-all-start.4) | async-done | bytes 2097184 | tf_op jit(solution)/shard_map/all_to_all | solution.py:73
  229.3 6.6 %shard_map.299.refs_4_ = bf16[2048,5376]{1,0:T(8,128)(2,1)} custom-call(s32[1]{0:T(128)} %bitcast.26.own_ref, bf16[128,5376]{1,0:T(8,128)(2,1)} %collective-permute-done.5.refs_0_, bf16[128,5376]{1,0:T(8,128)(2,1)} %collective-permute-done.23.refs_1_, bf16[128,5376]{1,0:T(8,128)(2,1)} %collective-permute-done.24.refs_2_, ...), custom_call_target="tpu_custom_call", output_to_operand_aliasing={{}: (7, {})} | custom-call | bytes 1048576 | tf_op jit(solution)/shard_map/pallas_call | solution.py:191
  235.9 8.5 %collective-permute-done.28.refs_0_ = bf16[64,5376]{1,0:T(8,128)(2,1)S(1)} collective-permute-done((bf16[64,5376]{1,0:T(8,128)(2,1)}, bf16[64,5376]{1,0:T(8,128)(2,1)S(1)}, u32[]{:S(2)}, u32[]{:S(2)}) %collective-permute-start.28) | collective-permute-done | bytes 688160 | tf_op jit(solution)/shard_map/ppermute | solution.py:82
  258.9 19.9 %shard_map.301 = (bf16[3,512,1792]{2,1,0:T(8,128)(2,1)}, bf16[2048,512]{1,0:T(8,128)(2,1)}) custom-call(s32[1]{0:T(128)} %bitcast.26.own_ref, bf16[512,2048]{1,0:T(8,128)(2,1)} %bitcast.147, bf16[512,2048]{1,0:T(8,128)(2,1)} %get-tuple-element.310.grad_ref, bf16[512,32]{1,0:T(8,128)(2,1)} %copy.173.gate_ref, bf16[32,1792]{1,0:T(8,128)(2,1)} %add_convert_fusion.7.spread_ref, ...), custom_call_target="tpu_custom_call" | custom-call | flops 11274289152 | bytes 33554432 | tf_op jit(solution)/shard_map/pallas_call | solution.py:816
  278.7 12.5 %shard_map.302 = bf16[512,2048]{1,0:T(8,128)(2,1)} custom-call(bf16[3,512,1792]{2,1,0:T(8,128)(2,1)} %get-tuple-element.338.hid_ref, bf16[2048,5376]{1,0:T(8,128)(2,1)} %shard_map.300.wg_ref.wu_ref.wd_ref.w_ref), custom_call_target="tpu_custom_call" | custom-call | flops 7516192768 | bytes 20971520 | tf_op jit(solution)/shard_map/pallas_call | solution.py:850
  291.3 7.6 %shard_map.303 = bf16[512,5376]{1,0:T(8,128)(2,1)} custom-call(bf16[2048,512]{1,0:T(8,128)(2,1)} %get-tuple-element.345.mid_ref, bf16[2048,512]{1,0:T(8,128)(2,1)} %get-tuple-element.321.grad_ref, bf16[3,512,1792]{2,1,0:T(8,128)(2,1)} %get-tuple-element.338.hid_ref), custom_call_target="tpu_custom_call" | custom-call | flops 58720256 | bytes 1048576 | tf_op jit(solution)/shard_map/pallas_call | solution.py:1048
  308.3 9.2 %shard_map.304 = (bf16[128,5376]{1,0:T(8,128)(2,1)}, bf16[128,5376]{1,0:T(8,128)(2,1)}, bf16[64,5376]{1,0:T(8,128)(2,1)}, bf16[64,5376]{1,0:T(8,128)(2,1)}, bf16[128,5376]{1,0:T(8,128)(2,1)}) custom-call(bf16[2048,512]{1,0:T(8,128)(2,1)} %get-tuple-element.345.mid_ref, bf16[2048,512]{1,0:T(8,128)(2,1)} %get-tuple-element.321.grad_ref, ...), custom_call_target="tpu_custom_call" | custom-call | flops 58720256 | bytes 1048576 | tf_op jit(solution)/shard_map/pallas_call | solution.py:1065
  320.2 7.6 %shard_map.305 = bf16[512,5376]{1,0:T(8,128)(2,1)} custom-call(bf16[2048,512]{1,0:T(8,128)(2,1)} %get-tuple-element.345.mid_ref, bf16[2048,512]{1,0:T(8,128)(2,1)} %get-tuple-element.321.grad_ref, bf16[3,512,1792]{2,1,0:T(8,128)(2,1)} %get-tuple-element.338.hid_ref), custom_call_target="tpu_custom_call" | custom-call | flops 58720256 | bytes 1048576 | tf_op jit(solution)/shard_map/pallas_call | solution.py:1048
  327.9 7.0 %all-to-all-done.6.parts_ref = bf16[8,64,2048]{2,1,0:T(8,128)(2,1)S(1)} async-done(((bf16[8,64,2048]{2,1,0:T(8,128)(2,1)}), bf16[8,64,2048]{2,1,0:T(8,128)(2,1)S(1)}, u32[]{:S(2)}, u32[]{:S(2)}) %all-to-all-start.6) | async-done | bytes 2097184 | tf_op jit(solution)/shard_map/all_to_all | solution.py:73
  347.0 11.2 %shard_map.307 = bf16[8,512,256]{2,1,0:T(8,128)(2,1)} custom-call(s32[1]{0:T(128)} %bitcast.col_ref, bf16[3,512,1792]{2,1,0:T(8,128)(2,1)} %get-tuple-element.338.hid_ref, bf16[2048,5376]{1,0:T(8,128)(2,1)} %shard_map.300.wg_ref.wu_ref.wd_ref.w_ref, f32[64,2048]{1,0:T(8,128)} %copy-done.6), custom_call_target="tpu_custom_call" | custom-call | flops 234881024 | bytes 1048576 | tf_op jit(solution)/shard_map/pallas_call | solution.py:875
  358.2 9.2 %shard_map.309 = (bf16[128,5376]{1,0:T(8,128)(2,1)}, bf16[128,5376]{1,0:T(8,128)(2,1)}, bf16[64,5376]{1,0:T(8,128)(2,1)}, bf16[64,5376]{1,0:T(8,128)(2,1)}, bf16[128,5376]{1,0:T(8,128)(2,1)}) custom-call(bf16[2048,512]{1,0:T(8,128)(2,1)} %get-tuple-element.345.mid_ref, bf16[2048,512]{1,0:T(8,128)(2,1)} %get-tuple-element.321.grad_ref, ...), custom_call_target="tpu_custom_call" | custom-call | flops 58720256 | bytes 1048576 | tf_op jit(solution)/shard_map/pallas_call | solution.py:1065
  367.4 10.5 %collective-permute-done.35 = bf16[128,5376]{1,0:T(8,128)(2,1)S(1)} collective-permute-done((bf16[128,5376]{1,0:T(8,128)(2,1)}, bf16[128,5376]{1,0:T(8,128)(2,1)S(1)}, u32[]{:S(2)}, u32[]{:S(2)}) %collective-permute-start.35) | collective-permute-done | bytes 1376288 | tf_op jit(solution)/shard_map/ppermute | solution.py:82
  403.2 10.0 %shard_map.311 = (bf16[256,256]{1,0:T(8,128)(2,1)}, bf16[256,256]{1,0:T(8,128)(2,1)}, bf16[256,256]{1,0:T(8,128)(2,1)}, bf16[256,256]{1,0:T(8,128)(2,1)}, bf16[1...) custom-call(s32[15]{0:T(128)} %pad_add_fusion.meta, bf16[256,256]{1,0:T(8,128)(2,1)} %get-tuple-element.270.q0.refs_0_, ...), custom_call_target="tpu_custom_call" | custom-call | flops 3489660928 | bytes 10485760 | tf_op jit(solution)/shard_map/pallas_call | solution.py:500
  443.1 8.1 %shard_map.314 = (bf16[8,128,640]{2,1,0:T(8,128)(2,1)}, bf16[8,128,640]{2,1,0:T(8,128)(2,1)}) custom-call(s32[1]{0:T(128)} %bitcast.26.own_ref, bf16[512,2048]{1,0:T(8,128)(2,1)} %get-tuple-element.394.normed_ref.x_ref, bf16[512,384]{1,0:T(8,128)(2,1)} %shard_map.313.dq_ref, bf16[512,2048]{1,0:T(8,128)(2,1)} %bitcast.145, ...), custom_call_target="tpu_custom_call" | custom-call | flops 16777216 | bytes 1048576 | tf_op jit(solution)/shard_map/pallas_call | solution.py:275
  451.2 6.6 %all-to-all-done.8.pack_ref = bf16[16,128,384]{2,1,0:T(8,128)(2,1)} async-done(((bf16[16,128,384]{2,1,0:T(8,128)(2,1)}), bf16[16,128,384]{2,1,0:T(8,128)(2,1)}, u32[]{:S(2)}, u32[]{:S(2)}) %all-to-all-start.8) | async-done | bytes 1572896 | tf_op jit(solution)/shard_map/all_to_all | solution.py:73
  487.7 8.0 %shard_map.316 = (bf16[8,512,256]{2,1,0:T(8,128)(2,1)}, f32[1,2048]{1,0:T(1,128)}) custom-call(s32[1]{0:T(128)} %bitcast.col_ref, bf16[512,384]{1,0:T(8,128)(2,1)} %shard_map.313.dq_ref, bf16[512,128]{1,0:T(8,128)(2,1)} %pad_bitcast_fusion.dl_ref, bf16[2048,896]{1,0:T(8,128)(2,1)} %bitcast.136, bf16[2048,896]{1,0:T(8,128)(2,1)} %bitcast.137, ...), custom_call_target="tpu_custom_call" | custom-call | flops 1342177280 | bytes 9437184 | tf_op jit(solution)/shard_map/pallas_call | solution.py:978
  501.9 7.0 %shard_map.317 = (bf16[8,128,256]{2,1,0:T(8,128)(2,1)}, bf16[8,128,256]{2,1,0:T(8,128)(2,1)}) custom-call(s32[1]{0:T(128)} %bitcast.26.own_ref, bf16[512,2048]{1,0:T(8,128)(2,1)} %get-tuple-element.394.normed_ref.x_ref, bf16[512,128]{1,0:T(8,128)(2,1)} %pad_bitcast_fusion.dl_ref, bf16[512,512]{1,0:T(8,128)(2,1)} %copy-done.12, ...), custom_call_target="tpu_custom_call" | custom-call | flops 16777216 | bytes 1048576 | tf_op jit(solution)/shard_map/pallas_call | solution.py:275
  521.6 10.5 %all-to-all-done.10 = bf16[8,512,256]{2,1,0:T(8,128)(2,1)} async-done(((bf16[8,512,256]{2,1,0:T(8,128)(2,1)}), bf16[8,512,256]{2,1,0:T(8,128)(2,1)}, u32[]{:S(2)}, u32[]{:S(2)}) %all-to-all-start.10) | async-done | bytes 2097184 | tf_op jit(solution)/shard_map/all_to_all | solution.py:73
  553.0 7.1 %collective-permute-done.61 = bf16[2,128,256]{2,1,0:T(8,128)(2,1)} collective-permute-done((bf16[2,128,256]{2,1,0:T(8,128)(2,1)}, bf16[2,128,256]{2,1,0:T(8,128)(2,1)}, u32[]{:S(2)}, u32[]{:S(2)}) %collective-permute-start.61) | collective-permute-done | bytes 131104 | tf_op jit(solution)/shard_map/ppermute | solution.py:82
  (371 shorter events, 347.7 us)
Async XLA Ops:
  21.5 37.1 %all-to-all-start = ((bf16[4,2,512,256]{3,2,1,0:T(8,128)(2,1)}), bf16[4,2,512,256]{3,2,1,0:T(8,128)(2,1)S(1)}, u32[]{:S(2)}, u32[]{:S(2)}) async-start(bf16[4,2,512,256]{3,2,1,0:T(8,128)(2,1)} %broadcast_in_dim.60), calls=%async_computation | async-start | bytes 4194304 | tf_op jit(solution)/shard_map/all_to_all | solution.py:73
  25.9 32.6 %collective-permute-start.5 = (bf16[128,5376]{1,0:T(8,128)(2,1)}, bf16[128,5376]{1,0:T(8,128)(2,1)}, u32[]{:S(2)}, u32[]{:S(2)}) collective-permute-start(bf16[128,5376]{1,0:T(8,128)(2,1)} %concatenate.39.refs_0_), channel_id=1, source_target_pairs={{0,64},{8,72},{16,80},{24,88},{32,96},{40,104},{48,112},{56,120},{... | collective-permute-start | bytes 4128776 | tf_op jit(solution)/shard_map/ppermute | solution.py:82
  61.6 32.9 %collective-permute-start.7 = (bf16[128,5376]{1,0:T(8,128)(2,1)}, bf16[128,5376]{1,0:T(8,128)(2,1)}, u32[]{:S(2)}, u32[]{:S(2)}) collective-permute-start(bf16[128,5376]{1,0:T(8,128)(2,1)} %concatenate.39.refs_0_), channel_id=1, source_target_pairs={{0,16},{8,24},{16,0},{24,8},{32,48},{40,56},{48,32},{56,40},{64,80... | collective-permute-start | bytes 4128776 | tf_op jit(solution)/shard_map/ppermute | solution.py:82
  63.2 33.7 %collective-permute-start.8 = (bf16[128,5376]{1,0:T(8,128)(2,1)}, bf16[128,5376]{1,0:T(8,128)(2,1)S(1)}, u32[]{:S(2)}, u32[]{:S(2)}) collective-permute-start(bf16[128,5376]{1,0:T(8,128)(2,1)} %concatenate.39.refs_0_), channel_id=1, source_target_pairs={{0,48},{8,56},{16,32},{24,40},{32,16},{40,24},{48,0},{56,8},{64,11... | collective-permute-start | bytes 4128776 | tf_op jit(solution)/shard_map/ppermute | solution.py:82
  100.3 34.3 %all-to-all-start.2 = ((bf16[16,128,384]{2,1,0:T(8,128)(2,1)}), bf16[16,128,384]{2,1,0:T(8,128)(2,1)}, u32[]{:S(2)}, u32[]{:S(2)}) async-start(bf16[16,128,384]{2,1,0:T(8,128)(2,1)} %get-tuple-element.262), calls=%async_computation.2 | async-start | bytes 3145728 | tf_op jit(solution)/shard_map/all_to_all | solution.py:73
  134.6 36.2 %all-to-all-start.3 = ((bf16[8,512,256]{2,1,0:T(8,128)(2,1)}), bf16[8,512,256]{2,1,0:T(8,128)(2,1)S(1)}, u32[]{:S(2)}, u32[]{:S(2)}) async-start(bf16[8,512,256]{2,1,0:T(8,128)(2,1)} %broadcast_in_dim.63), calls=%async_computation.3 | async-start | bytes 4194304 | tf_op jit(solution)/shard_map/all_to_all | solution.py:73
  142.3 42.0 %collective-permute-start.18 = (bf16[128,5376]{1,0:T(8,128)(2,1)}, bf16[128,5376]{1,0:T(8,128)(2,1)}, u32[]{:S(2)}, u32[]{:S(2)}) collective-permute-start(bf16[128,5376]{1,0:T(8,128)(2,1)} %concatenate.39.refs_0_), channel_id=1, source_target_pairs={{0,8},{8,0},{16,24},{24,16},{32,40},{40,32},{48,56},{56,48},{64,72... | collective-permute-start | bytes 4128776 | tf_op jit(solution)/shard_map/ppermute | solution.py:82
  142.6 41.8 %collective-permute-start.19 = (bf16[128,5376]{1,0:T(8,128)(2,1)}, bf16[128,5376]{1,0:T(8,128)(2,1)}, u32[]{:S(2)}, u32[]{:S(2)}) collective-permute-start(bf16[128,5376]{1,0:T(8,128)(2,1)} %collective-permute-done.7.refs_1_), channel_id=1, source_target_pairs={{0,8},{8,0},{16,24},{24,16},{32,40},{40,32},{48,56},{56,48},{64,72... | collective-permute-start | bytes 4128776 | tf_op jit(solution)/shard_map/ppermute | solution.py:82
  175.7 32.8 %all-to-all-start.4 = ((bf16[8,64,2048]{2,1,0:T(8,128)(2,1)}), bf16[8,64,2048]{2,1,0:T(8,128)(2,1)S(1)}, u32[]{:S(2)}, u32[]{:S(2)}) async-start(bf16[8,64,2048]{2,1,0:T(8,128)(2,1)} %get-tuple-element.294), calls=%async_computation.4 | async-start | bytes 4194304 | tf_op jit(solution)/shard_map/all_to_all | solution.py:73
  181.2 32.9 %collective-permute-start.23 = (bf16[128,5376]{1,0:T(8,128)(2,1)}, bf16[128,5376]{1,0:T(8,128)(2,1)}, u32[]{:S(2)}, u32[]{:S(2)}) collective-permute-start(bf16[128,5376]{1,0:T(8,128)(2,1)} %collective-permute-done.5.refs_0_), channel_id=1, source_target_pairs={{0,16},{8,24},{16,0},{24,8},{32,48},{40,56},{48,32},{56,40},{64,80... | collective-permute-start | bytes 4128776 | tf_op jit(solution)/shard_map/ppermute | solution.py:82
  182.4 33.8 %collective-permute-start.24 = (bf16[128,5376]{1,0:T(8,128)(2,1)}, bf16[128,5376]{1,0:T(8,128)(2,1)}, u32[]{:S(2)}, u32[]{:S(2)}) collective-permute-start(bf16[128,5376]{1,0:T(8,128)(2,1)} %collective-permute-done.5.refs_0_), channel_id=1, source_target_pairs={{0,48},{8,56},{16,32},{24,40},{32,16},{40,24},{48,0},{56,8},{64,11... | collective-permute-start | bytes 4128776 | tf_op jit(solution)/shard_map/ppermute | solution.py:82
  216.2 35.9 %all-to-all-start.5 = ((bf16[8,64,2048]{2,1,0:T(8,128)(2,1)}), bf16[8,64,2048]{2,1,0:T(8,128)(2,1)S(1)}, u32[]{:S(2)}, u32[]{:S(2)}) async-start(bf16[8,64,2048]{2,1,0:T(8,128)(2,1)} %copy-done.8), calls=%async_computation.5 | async-start | bytes 4194304 | tf_op jit(solution)/shard_map/all_to_all | solution.py:73
  299.0 35.8 %all-to-all-start.6 = ((bf16[8,64,2048]{2,1,0:T(8,128)(2,1)}), bf16[8,64,2048]{2,1,0:T(8,128)(2,1)S(1)}, u32[]{:S(2)}, u32[]{:S(2)}) async-start(bf16[8,64,2048]{2,1,0:T(8,128)(2,1)} %bitcast.146), calls=%async_computation.6 | async-start | bytes 4194304 | tf_op jit(solution)/shard_map/all_to_all | solution.py:73
  337.7 41.8 %all-to-all-start.7 = ((bf16[8,64,2048]{2,1,0:T(8,128)(2,1)}), bf16[8,64,2048]{2,1,0:T(8,128)(2,1)S(1)}, u32[]{:S(2)}, u32[]{:S(2)}) async-start(bf16[8,64,2048]{2,1,0:T(8,128)(2,1)} %copy-done.7), calls=%async_computation.7 | async-start | bytes 4194304 | tf_op jit(solution)/shard_map/all_to_all | solution.py:73
  345.2 32.8 %collective-permute-start.35 = (bf16[128,5376]{1,0:T(8,128)(2,1)}, bf16[128,5376]{1,0:T(8,128)(2,1)S(1)}, u32[]{:S(2)}, u32[]{:S(2)}) collective-permute-start(bf16[128,5376]{1,0:T(8,128)(2,1)} %get-tuple-element.343), channel_id=1, source_target_pairs={{0,16},{8,24},{16,0},{24,8},{32,48},{40,56},{48,32},{56,40},{64,80... | collective-permute-start | bytes 4128776 | tf_op jit(solution)/shard_map/ppermute | solution.py:82
  345.2 34.3 %collective-permute-start.36 = (bf16[128,5376]{1,0:T(8,128)(2,1)}, bf16[128,5376]{1,0:T(8,128)(2,1)}, u32[]{:S(2)}, u32[]{:S(2)}) collective-permute-start(bf16[128,5376]{1,0:T(8,128)(2,1)} %get-tuple-element.344), channel_id=1, source_target_pairs={{0,48},{8,56},{16,32},{24,40},{32,16},{40,24},{48,0},{56,8},{64,11... | collective-permute-start | bytes 4128776 | tf_op jit(solution)/shard_map/ppermute | solution.py:82
  429.4 28.4 %all-to-all-start.8 = ((bf16[16,128,384]{2,1,0:T(8,128)(2,1)}), bf16[16,128,384]{2,1,0:T(8,128)(2,1)}, u32[]{:S(2)}, u32[]{:S(2)}) async-start(bf16[16,128,384]{2,1,0:T(8,128)(2,1)} %add_convert_fusion), calls=%async_computation.8 | async-start | bytes 3145728 | tf_op jit(solution)/shard_map/all_to_all | solution.py:73
  457.8 39.1 %collective-permute-start.52 = (bf16[128,5376]{1,0:T(8,128)(2,1)}, bf16[128,5376]{1,0:T(8,128)(2,1)}, u32[]{:S(2)}, u32[]{:S(2)}) collective-permute-start(bf16[128,5376]{1,0:T(8,128)(2,1)} %get-tuple-element.409), channel_id=1, source_target_pairs={{0,16},{8,24},{16,0},{24,8},{32,48},{40,56},{48,32},{56,40},{64,80... | collective-permute-start | bytes 4128776 | tf_op jit(solution)/shard_map/ppermute | solution.py:82
  457.8 39.1 %collective-permute-start.53 = (bf16[128,5376]{1,0:T(8,128)(2,1)}, bf16[128,5376]{1,0:T(8,128)(2,1)}, u32[]{:S(2)}, u32[]{:S(2)}) collective-permute-start(bf16[128,5376]{1,0:T(8,128)(2,1)} %get-tuple-element.410), channel_id=1, source_target_pairs={{0,48},{8,56},{16,32},{24,40},{32,16},{40,24},{48,0},{56,8},{64,11... | collective-permute-start | bytes 4128776 | tf_op jit(solution)/shard_map/ppermute | solution.py:82
  482.9 38.6 %collective-permute-start.55 = (bf16[2,128,640]{2,1,0:T(8,128)(2,1)}, bf16[2,128,640]{2,1,0:T(8,128)(2,1)}, u32[]{:S(2)}, u32[]{:S(2)}) collective-permute-start(bf16[2,128,640]{2,1,0:T(8,128)(2,1)} %get-tuple-element.538), channel_id=1, source_target_pairs={{0,16},{8,24},{16,0},{24,8},{32,48},{40,56},{48,32},{56,40},{64,80... | collective-permute-start | bytes 983048 | tf_op jit(solution)/shard_map/ppermute | solution.py:82
  484.3 37.2 %collective-permute-start.56 = (bf16[2,128,640]{2,1,0:T(8,128)(2,1)}, bf16[2,128,640]{2,1,0:T(8,128)(2,1)}, u32[]{:S(2)}, u32[]{:S(2)}) collective-permute-start(bf16[2,128,640]{2,1,0:T(8,128)(2,1)} %get-tuple-element.537), channel_id=1, source_target_pairs={{0,32},{8,40},{16,48},{24,56},{32,0},{40,8},{48,16},{56,24},{64,96... | collective-permute-start | bytes 983048 | tf_op jit(solution)/shard_map/ppermute | solution.py:82
  495.7 25.9 %collective-permute-start.57 = (bf16[2,128,640]{2,1,0:T(8,128)(2,1)}, bf16[2,128,640]{2,1,0:T(8,128)(2,1)}, u32[]{:S(2)}, u32[]{:S(2)}) collective-permute-start(bf16[2,128,640]{2,1,0:T(8,128)(2,1)} %get-tuple-element.536), channel_id=1, source_target_pairs={{0,48},{8,56},{16,32},{24,40},{32,16},{40,24},{48,0},{56,8},{64,11... | collective-permute-start | bytes 983048 | tf_op jit(solution)/shard_map/ppermute | solution.py:82
  496.9 35.2 %all-to-all-start.10 = ((bf16[8,512,256]{2,1,0:T(8,128)(2,1)}), bf16[8,512,256]{2,1,0:T(8,128)(2,1)}, u32[]{:S(2)}, u32[]{:S(2)}) async-start(bf16[8,512,256]{2,1,0:T(8,128)(2,1)} %get-tuple-element.413), calls=%async_computation.10 | async-start | bytes 4194304 | tf_op jit(solution)/shard_map/all_to_all | solution.py:73
  533.3 37.2 %all-to-all-start.11 = ((bf16[128,36,128]{2,1,0:T(8,128)(2,1)}), bf16[128,36,128]{2,1,0:T(8,128)(2,1)S(1)}, u32[]{:S(2)}, u32[]{:S(2)}) async-start(bf16[128,36,128]{2,1,0:T(8,128)(2,1)} %broadcast_in_dim.71), calls=%async_computation.11 | async-start | bytes 2621440 | tf_op jit(solution)/shard_map/all_to_all | solution.py:73
  (105 other events, 1339.9 us)
